TPU v7x, 512 devices: a whole 4x4x16 slice. The times are simulated.
512 devices in a mesh: pipe: 32 (over z_lo, y, core), tensor: 16 (over z_hi, x).
Axes of the slice: x: 4, y: 4, z: 16 (z_hi: 4, z_lo: 4; z = z_hi * 4 + z_lo), core: 2. Of those that a mesh axis runs over, the one named last changes fastest.
Arguments:
- fwd_qkv: bfloat16 [32, 896, 32, 384], P('pipe', None, 'tensor'), may hold values from -5 to 5
- held_stash: bfloat16 [32, 896, 32, 384], P('pipe', 'tensor'), may hold values from -5 to 5
- d_out: bfloat16 [32, 896, 32, 128], P('pipe', None, 'tensor'), may hold values from -6 to 6
- positions: int32 [4, 896], replicated, may hold values from 0 to 895, as said below
- plan: int32 [32, 2], P('pipe'), may hold values from 0 to 3
Outputs:
- to_next: bfloat16 [32, 896, 32, 128], P('pipe', None, 'tensor')
- to_prev: bfloat16 [32, 896, 32, 384], P('pipe', None, 'tensor')
Inputs may be any that keep to these rules, and one draw needn't show every extreme that they name: `positions`: row 0 of every micro-batch starts a document; a position is 0 where a document starts and one more than the row before otherwise; one micro-batch is a single document.
All inputs are finite; a program needn't handle non-finite values.
Results may differ from a plain program's by a relative error of at most 0.0064.
Values may be sent and summed in bfloat16 or wider, within the bound.
No kernel may reach another device: no remote copies, remote signals or barrier semaphores. Data moves between devices by JAX's collectives and lax.ppermute only.
A program may use at most 64 MiB of HBM per device.

v0:
```python
import jax
import jax.numpy as jnp
from jax import lax
from jax.sharding import PartitionSpec as P


def from_partner(block, axis, distance):
    count = lax.axis_size(axis)
    route = []
    for low in range(count):
        high = low | 1 << distance
        if high != low and high < count:
            route += [(low, high), (high, low)]
    return lax.ppermute(block, axis, route)


def passed_along(block, axis, distance):
    devices = range(lax.axis_size(axis))
    route = [(i - distance, i) for i in devices if i - distance in devices]
    return lax.ppermute(block, axis, route)


def visible_of(pos):
    count = pos.shape[0]
    rows = lax.broadcasted_iota(jnp.int32, (count, count), 0)
    cols = lax.broadcasted_iota(jnp.int32, (count, count), 1)
    return (cols <= rows) & (cols >= rows - pos[:, None])


def probabilities(query, keys, pos):
    scale = query.shape[-1] ** (-0.5)
    scores = jnp.einsum("thd,shd->hts", query, keys, preferred_element_type=jnp.float32) * scale
    scores = jnp.where(visible_of(pos)[None], scores, -jnp.inf)
    top = jnp.max(scores, axis=-1, keepdims=True)
    expo = jnp.exp(scores - top)
    return expo / jnp.sum(expo, axis=-1, keepdims=True)


def forward_of(packed, pos):
    width = packed.shape[-1] // 3
    probs = probabilities(packed[..., :width], packed[..., width : 2 * width], pos)
    weights = probs.astype(jnp.bfloat16)
    result = jnp.einsum(
        "hts,shd->thd", weights, packed[..., 2 * width :], preferred_element_type=jnp.float32
    )
    return result.astype(jnp.bfloat16)


def backward_of(packed, pos, grad_out):
    width = packed.shape[-1] // 3
    scale = width ** (-0.5)
    query = packed[..., :width]
    keys = packed[..., width : 2 * width]
    values = packed[..., 2 * width :]
    probs = probabilities(query, keys, pos)
    weights = probs.astype(jnp.bfloat16)
    grad_values = jnp.einsum("hts,thd->shd", weights, grad_out, preferred_element_type=jnp.float32)
    grad_probs = jnp.einsum("thd,shd->hts", grad_out, values, preferred_element_type=jnp.float32)
    delta = jnp.sum(probs * grad_probs, axis=-1, keepdims=True)
    grad_scores = (probs * (grad_probs - delta) * scale).astype(jnp.bfloat16)
    grad_query = jnp.einsum("hts,shd->thd", grad_scores, keys, preferred_element_type=jnp.float32)
    grad_keys = jnp.einsum("hts,thd->shd", grad_scores, query, preferred_element_type=jnp.float32)
    return jnp.concatenate(
        [
            grad_query.astype(jnp.bfloat16),
            grad_keys.astype(jnp.bfloat16),
            grad_values.astype(jnp.bfloat16),
        ],
        axis=-1,
    )


def from_mirror(block):
    moved = block
    for bit_number in range(lax.axis_size("pipe").bit_length() - 1):
        moved = from_partner(moved, "pipe", bit_number)
    return moved


def local(fwd_qkv, held_stash, d_out, positions, plan):
    forward_pos = lax.dynamic_index_in_dim(positions, plan[0, 0], 0, keepdims=False)
    backward_pos = lax.dynamic_index_in_dim(positions, plan[0, 1], 0, keepdims=False)
    holding = held_stash[0]
    fetched = from_mirror(holding)
    stash = lax.all_to_all(fetched, "tensor", split_axis=1, concat_axis=0, tiled=True)
    result = forward_of(fwd_qkv[0], forward_pos)
    grads = backward_of(stash, backward_pos, d_out[0])
    to_next = passed_along(result[None], "pipe", 1)
    to_prev = passed_along(grads[None], "pipe", -1)
    return (to_next, to_prev)


def solution(mesh):
    placed = (
        P("pipe", None, "tensor", None),
        P("pipe", "tensor", None, None),
        P("pipe", None, "tensor", None),
        P(),
        P("pipe", None),
    )
    return jax.shard_map(
        local,
        mesh=mesh,
        in_specs=placed,
        out_specs=(P("pipe", None, "tensor", None), P("pipe", None, "tensor", None)),
        check_vma=False,
    )
```

profile of v0, /device:TPU:36, one launch (start us, length us, event | category | flops | bytes accessed | tf_op | source)
XLA Modules:
  0.0 321.3 jit_solution(1239065931578494419)
XLA Ops:
  0.6 0.0 copy-start
  0.6 0.0 copy-start.4
  0.6 1.9 copy.40
  2.6 1.9 collective-permute-start.1
  4.5 3.1 collective-permute-done.1
  7.6 3.5 %collective-permute-start.2 = (bf16[56,32,384]{2,0,1:T(8,128)(2,1)S(1)}, bf16[56,32,384]{2,0,1:T(8,128)(2,1)S(1)}, u32[]{:S(2)}, u32[]{:S(2)}) collective-permute-start(bf16[56,32,384]{2,0,1:T(8,128)(2,1)S(1)} %collective-permute-done.1), channel_id=1, source_target_pairs={{0,32},{32,0},{16,48},{48,16},{64,96},{96,64},{80,112},{112,80},{1... | collective-permute-start | bytes 4128776 | tf_op jit(solution)/shard_map/ppermute | solution.py:14
  11.1 30.6 %collective-permute-done.2 = bf16[56,32,384]{2,0,1:T(8,128)(2,1)S(1)} collective-permute-done((bf16[56,32,384]{2,0,1:T(8,128)(2,1)S(1)}, bf16[56,32,384]{2,0,1:T(8,128)(2,1)S(1)}, u32[]{:S(2)}, u32[]{:S(2)}) %collective-permute-start.2) | collective-permute-done | bytes 1376288 | tf_op jit(solution)/shard_map/ppermute | solution.py:14
  41.7 5.1 %collective-permute-start.3 = (bf16[56,32,384]{2,0,1:T(8,128)(2,1)S(1)}, bf16[56,32,384]{2,0,1:T(8,128)(2,1)S(1)}, u32[]{:S(2)}, u32[]{:S(2)}) collective-permute-start(bf16[56,32,384]{2,0,1:T(8,128)(2,1)S(1)} %collective-permute-done.2), channel_id=1, source_target_pairs={{0,64},{64,0},{16,80},{80,16},{32,96},{96,32},{48,112},{112,48},{1... | collective-permute-start | bytes 4128776 | tf_op jit(solution)/shard_map/ppermute | solution.py:14
  46.8 29.7 %collective-permute-done.3 = bf16[56,32,384]{2,0,1:T(8,128)(2,1)S(1)} collective-permute-done((bf16[56,32,384]{2,0,1:T(8,128)(2,1)S(1)}, bf16[56,32,384]{2,0,1:T(8,128)(2,1)S(1)}, u32[]{:S(2)}, u32[]{:S(2)}) %collective-permute-start.3) | collective-permute-done | bytes 1376288 | tf_op jit(solution)/shard_map/ppermute | solution.py:14
  76.5 2.0 collective-permute-start.4
  78.5 30.3 %collective-permute-done.4 = bf16[56,32,384]{2,0,1:T(8,128)(2,1)S(1)} collective-permute-done((bf16[56,32,384]{2,0,1:T(8,128)(2,1)S(1)}, bf16[56,32,384]{2,0,1:T(8,128)(2,1)S(1)}, u32[]{:S(2)}, u32[]{:S(2)}) %collective-permute-start.4) | collective-permute-done | bytes 1376288 | tf_op jit(solution)/shard_map/ppermute | solution.py:14
  108.8 5.2 %collective-permute-start.5 = (bf16[56,32,384]{2,0,1:T(8,128)(2,1)S(1)}, bf16[56,32,384]{2,0,1:T(8,128)(2,1)}, u32[]{:S(2)}, u32[]{:S(2)}) collective-permute-start(bf16[56,32,384]{2,0,1:T(8,128)(2,1)S(1)} %collective-permute-done.4), channel_id=1, source_target_pairs={{0,256},{256,0},{16,272},{272,16},{32,288},{288,32},{48,304},{304,... | collective-permute-start | bytes 4128776 | tf_op jit(solution)/shard_map/ppermute | solution.py:14
  114.0 56.5 %collective-permute-done.5 = bf16[56,32,384]{2,0,1:T(8,128)(2,1)} collective-permute-done((bf16[56,32,384]{2,0,1:T(8,128)(2,1)S(1)}, bf16[56,32,384]{2,0,1:T(8,128)(2,1)}, u32[]{:S(2)}, u32[]{:S(2)}) %collective-permute-start.5) | collective-permute-done | bytes 1376288 | tf_op jit(solution)/shard_map/ppermute | solution.py:14
  170.5 15.5 %all-to-all-start = ((bf16[56,32,384]{2,0,1:T(8,128)(2,1)}), bf16[56,32,384]{2,0,1:T(8,128)(2,1)S(1)}, u32[]{:S(2)}, u32[]{:S(2)}) async-start(bf16[56,32,384]{2,0,1:T(8,128)(2,1)} %collective-permute-done.5), calls=%async_computation | async-start | bytes 2752512 | tf_op jit(solution)/shard_map/all_to_all | solution.py:85
  185.9 1.3 fusion.84
  189.8 1.4 copy.29
  191.2 0.0 copy-done
  191.2 1.3 copy.41
  193.8 0.0 copy-done.4
  193.9 1.3 fusion.20
  195.2 1.4 fusion.21
  196.6 42.7 %all-to-all-done = bf16[56,32,384]{2,0,1:T(8,128)(2,1)S(1)} async-done(((bf16[56,32,384]{2,0,1:T(8,128)(2,1)}), bf16[56,32,384]{2,0,1:T(8,128)(2,1)S(1)}, u32[]{:S(2)}, u32[]{:S(2)}) %all-to-all-start) | async-done | bytes 1376288 | tf_op jit(solution)/shard_map/all_to_all | solution.py:85
  239.2 0.1 copy.22
  239.4 6.2 %fusion.94 = (f32[2,896]{1,0:T(2,128)S(1)}, f32[2,896,896]{1,2,0:T(8,128)}) fusion(pred[896,896]{0,1:T(8,128)(4,1)} %fusion.20, bf16[896,2,384]{2,0,1:T(8,128)(2,1)S(1)} %bitcast.28), kind=kOutput, calls=%fused_computation.72 | convolution fusion | flops 417465216 | bytes 8150016 | tf_op jit(solution)/shard_map/sub | solution.py:35
  245.5 3.7 %fusion.49 = f32[2,896,896]{1,2,0:T(8,128)} fusion(bf16[896,2,128]{0,2,1:T(8,128)(2,1)S(1)} %copy.29, bf16[896,2,384]{2,0,1:T(8,128)(2,1)S(1)} %bitcast.29), kind=kOutput, calls=%fused_computation.43 | convolution fusion | flops 411041792 | bytes 7340032 | tf_op jit(solution)/shard_map/thd,shd->hts/dot_general | solution.py:58
  249.2 11.1 %fusion.39 = bf16[896,2,128]{0,2,1:T(8,128)(2,1)} fusion(f32[2,896,896]{1,2,0:T(8,128)} %fusion.49, bf16[896,2,384]{2,0,1:T(8,128)(2,1)S(1)} %bitcast.30, f32[2,896,896]{1,2,0:T(8,128)} %get-tuple-element.13, f32[2,896]{1,0:T(2,128)S(1)} %get-tuple-element.12), kind=kOutput, calls=%fused_computation.39 | convolution fusion | flops 422513280 | bytes 26621952 | tf_op jit(solution)/shard_map/hts,shd->thd/dot_general | solution.py:61
  260.3 11.2 %fusion.36 = bf16[896,2,128]{0,2,1:T(8,128)(2,1)} fusion(f32[2,896,896]{1,2,0:T(8,128)} %fusion.49, bf16[896,2,384]{2,0,1:T(8,128)(2,1)S(1)} %bitcast.31, f32[2,896,896]{1,2,0:T(8,128)} %get-tuple-element.13, f32[2,896]{1,0:T(2,128)S(1)} %get-tuple-element.12), kind=kOutput, calls=%fused_computation.38 | convolution fusion | flops 422513280 | bytes 26621952 | tf_op jit(solution)/shard_map/hts,thd->shd/dot_general | solution.py:62
  271.5 0.0 copy-start.2
  271.5 0.0 copy-start.3
  271.5 0.0 copy-start.1
  271.5 4.1 %fusion.42 = bf16[896,2,128]{0,2,1:T(8,128)(2,1)S(1)} fusion(bf16[896,2,128]{0,2,1:T(8,128)(2,1)S(1)} %copy.29, f32[2,896,896]{1,2,0:T(8,128)} %get-tuple-element.13, f32[2,896]{1,0:T(2,128)S(1)} %get-tuple-element.12), kind=kOutput, calls=%fused_computation.40 | convolution fusion | flops 414482432 | bytes 7347200 | tf_op jit(solution)/shard_map/hts,thd->shd/dot_general | solution.py:57
  275.5 0.0 copy-done.2
  275.6 0.0 copy-done.3
  275.6 0.1 maximum_bitcast_fusion
  275.7 17.2 %collective-permute-start.6 = (bf16[1,896,2,384]{1,3,2,0:T(8,128)(2,1)S(1)}, bf16[1,896,2,384]{1,3,2,0:T(8,128)(2,1)}, u32[]{:S(2)}, u32[]{:S(2)}) collective-permute-start(bf16[1,896,2,384]{1,3,2,0:T(8,128)(2,1)S(1)} %maximum_bitcast_fusion), channel_id=1, source_target_pairs={{16,0},{32,16},{48,32},{64,48},{80,64},{96,80},{112,96},{128,112},... | collective-permute-start | bytes 4128776 | tf_op jit(solution)/shard_map/ppermute | solution.py:20
  292.9 0.0 copy-done.1
  292.9 6.2 %fusion.85 = (f32[2,896]{1,0:T(2,128)S(1)}, f32[2,896,896]{1,2,0:T(8,128)}) fusion(pred[896,896]{0,1:T(8,128)(4,1)} %fusion.21, bf16[896,2,384]{2,0,1:T(8,128)(2,1)S(1)} %bitcast.32), kind=kOutput, calls=%fused_computation.71 | convolution fusion | flops 417465216 | bytes 8150016 | tf_op jit(solution)/shard_map/sub | solution.py:35
  299.1 4.2 %fusion.35 = bf16[1,896,2,128]{3,1,2,0:T(8,128)(2,1)S(1)} fusion(f32[2,896,896]{1,2,0:T(8,128)} %get-tuple-element.11, f32[2,896]{1,0:T(2,128)S(1)} %get-tuple-element.10, bf16[896,2,384]{2,0,1:T(8,128)(2,1)S(1)} %bitcast.33), kind=kOutput, calls=%fused_computation.37 | convolution fusion | flops 414482432 | bytes 7347200 | tf_op jit(solution)/shard_map/hts,shd->thd/dot_general | solution.py:43
  303.3 1.9 collective-permute-start
  305.2 10.0 %collective-permute-done = bf16[1,896,2,128]{3,1,2,0:T(8,128)(2,1)S(1)} collective-permute-done((bf16[1,896,2,128]{3,1,2,0:T(8,128)(2,1)S(1)}, bf16[1,896,2,128]{3,1,2,0:T(8,128)(2,1)S(1)}, u32[]{:S(2)}, u32[]{:S(2)}) %collective-permute-start) | collective-permute-done | bytes 458784 | tf_op jit(solution)/shard_map/ppermute | solution.py:20
  315.2 1.2 copy.30
  316.4 0.0 collective-permute-done.6
  316.4 4.9 %copy.31 = bf16[1,896,2,384]{3,2,1,0:T(2,128)(2,1)} copy(bf16[1,896,2,384]{1,3,2,0:T(8,128)(2,1)} %collective-permute-done.6) | data formatting | bytes 2752512
  (3 shorter events, 0.0 us)
Async XLA Ops:
  0.6 190.6 %copy-start = (bf16[1,896,2,384]{3,2,1,0:T(2,128)(2,1)S(1)}, bf16[1,896,2,384]{3,2,1,0:T(2,128)(2,1)}, u32[]{:S(2)}) copy-start(bf16[1,896,2,384]{3,2,1,0:T(2,128)(2,1)} %param.5) | copy-start | bytes 4128772
  0.6 193.2 %copy-start.4 = (s32[4,896]{1,0:T(4,128)S(1)}, s32[4,896]{1,0:T(4,128)}, u32[]{:S(2)}) copy-start(s32[4,896]{1,0:T(4,128)} %param.8) | copy-start | bytes 43012
  2.6 5.0 %collective-permute-start.1 = (bf16[56,32,384]{2,0,1:T(8,128)(2,1)S(1)}, bf16[56,32,384]{2,0,1:T(8,128)(2,1)S(1)}, u32[]{:S(2)}, u32[]{:S(2)}) collective-permute-start(bf16[56,32,384]{2,0,1:T(8,128)(2,1)S(1)} %bitcast.34), channel_id=1, source_target_pairs={{0,16},{16,0},{32,48},{48,32},{64,80},{80,64},{96,112},{112,96},{1... | collective-permute-start | bytes 4128776 | tf_op jit(solution)/shard_map/ppermute | solution.py:14
  7.6 34.1 %collective-permute-start.2 = (bf16[56,32,384]{2,0,1:T(8,128)(2,1)S(1)}, bf16[56,32,384]{2,0,1:T(8,128)(2,1)S(1)}, u32[]{:S(2)}, u32[]{:S(2)}) collective-permute-start(bf16[56,32,384]{2,0,1:T(8,128)(2,1)S(1)} %collective-permute-done.1), channel_id=1, source_target_pairs={{0,32},{32,0},{16,48},{48,16},{64,96},{96,64},{80,112},{112,80},{1... | collective-permute-start | bytes 4128776 | tf_op jit(solution)/shard_map/ppermute | solution.py:14
  41.7 34.8 %collective-permute-start.3 = (bf16[56,32,384]{2,0,1:T(8,128)(2,1)S(1)}, bf16[56,32,384]{2,0,1:T(8,128)(2,1)S(1)}, u32[]{:S(2)}, u32[]{:S(2)}) collective-permute-start(bf16[56,32,384]{2,0,1:T(8,128)(2,1)S(1)} %collective-permute-done.2), channel_id=1, source_target_pairs={{0,64},{64,0},{16,80},{80,16},{32,96},{96,32},{48,112},{112,48},{1... | collective-permute-start | bytes 4128776 | tf_op jit(solution)/shard_map/ppermute | solution.py:14
  76.5 32.4 %collective-permute-start.4 = (bf16[56,32,384]{2,0,1:T(8,128)(2,1)S(1)}, bf16[56,32,384]{2,0,1:T(8,128)(2,1)S(1)}, u32[]{:S(2)}, u32[]{:S(2)}) collective-permute-start(bf16[56,32,384]{2,0,1:T(8,128)(2,1)S(1)} %collective-permute-done.3), channel_id=1, source_target_pairs={{0,128},{128,0},{16,144},{144,16},{32,160},{160,32},{48,176},{176,... | collective-permute-start | bytes 4128776 | tf_op jit(solution)/shard_map/ppermute | solution.py:14
  108.8 61.6 %collective-permute-start.5 = (bf16[56,32,384]{2,0,1:T(8,128)(2,1)S(1)}, bf16[56,32,384]{2,0,1:T(8,128)(2,1)}, u32[]{:S(2)}, u32[]{:S(2)}) collective-permute-start(bf16[56,32,384]{2,0,1:T(8,128)(2,1)S(1)} %collective-permute-done.4), channel_id=1, source_target_pairs={{0,256},{256,0},{16,272},{272,16},{32,288},{288,32},{48,304},{304,... | collective-permute-start | bytes 4128776 | tf_op jit(solution)/shard_map/ppermute | solution.py:14
  170.5 68.8 %all-to-all-start = ((bf16[56,32,384]{2,0,1:T(8,128)(2,1)}), bf16[56,32,384]{2,0,1:T(8,128)(2,1)S(1)}, u32[]{:S(2)}, u32[]{:S(2)}) async-start(bf16[56,32,384]{2,0,1:T(8,128)(2,1)} %collective-permute-done.5), calls=%async_computation | async-start | bytes 2752512 | tf_op jit(solution)/shard_map/all_to_all | solution.py:85
  271.5 4.1 %copy-start.2 = (bf16[896,2,128]{0,2,1:T(8,128)(2,1)S(1)}, bf16[896,2,128]{0,2,1:T(8,128)(2,1)}, u32[]{:S(2)}) copy-start(bf16[896,2,128]{0,2,1:T(8,128)(2,1)} %fusion.39) | copy-start | bytes 1376260
  271.5 4.1 %copy-start.3 = (bf16[896,2,128]{0,2,1:T(8,128)(2,1)S(1)}, bf16[896,2,128]{0,2,1:T(8,128)(2,1)}, u32[]{:S(2)}) copy-start(bf16[896,2,128]{0,2,1:T(8,128)(2,1)} %fusion.36) | copy-start | bytes 1376260
  271.5 21.4 %copy-start.1 = (bf16[1,896,2,384]{3,1,2,0:T(8,128)(2,1)S(1)}, bf16[1,896,2,384]{3,1,2,0:T(8,128)(2,1)}, u32[]{:S(2)}) copy-start(bf16[1,896,2,384]{3,1,2,0:T(8,128)(2,1)} %copy.41) | copy-start | bytes 4128772
  275.7 40.7 %collective-permute-start.6 = (bf16[1,896,2,384]{1,3,2,0:T(8,128)(2,1)S(1)}, bf16[1,896,2,384]{1,3,2,0:T(8,128)(2,1)}, u32[]{:S(2)}, u32[]{:S(2)}) collective-permute-start(bf16[1,896,2,384]{1,3,2,0:T(8,128)(2,1)S(1)} %maximum_bitcast_fusion), channel_id=1, source_target_pairs={{16,0},{32,16},{48,32},{64,48},{80,64},{96,80},{112,96},{128,112},... | collective-permute-start | bytes 4128776 | tf_op jit(solution)/shard_map/ppermute | solution.py:20
  303.3 11.9 %collective-permute-start = (bf16[1,896,2,128]{3,1,2,0:T(8,128)(2,1)S(1)}, bf16[1,896,2,128]{3,1,2,0:T(8,128)(2,1)S(1)}, u32[]{:S(2)}, u32[]{:S(2)}) collective-permute-start(bf16[1,896,2,128]{3,1,2,0:T(8,128)(2,1)S(1)} %fusion.35), channel_id=1, source_target_pairs={{0,16},{16,32},{32,48},{48,64},{64,80},{80,96},{96,112},{112,128},... | collective-permute-start | bytes 1376264 | tf_op jit(solution)/shard_map/ppermute | solution.py:20
where the time goes:
time: 322 us; the launch traced here: 321 us
  waiting for transfers between devices  203 us (63%)
  starting transfers between devices  52.2 us (16%)
  matrix products  46.5 us (14%)
  local copies, waits for them, and re-layouts  12.2 us (4%)
  between operations  4.66 us (1%)
    ppermute x5, waiting for transfers between devices, from_partner(): return lax.ppermute(block, axis, route)  150 us
    all_to_all x1, waiting for transfers between devices, local(): lax.all_to_all(fetched, 'tensor', split_axis=1, concat_axis=0, tiled=True)  42.7 us
    ppermute x2, starting transfers between devices, passed_along(): return lax.ppermute(block, axis, route)  19.1 us
    ppermute x5, starting transfers between devices, from_partner(): return lax.ppermute(block, axis, route)  17.7 us
    all_to_all x1, starting transfers between devices, local(): lax.all_to_all(fetched, 'tensor', split_axis=1, concat_axis=0, tiled=True)  15.5 us
    sub x2, matrix products, probabilities(): expo = jnp.exp(scores - top)  12.3 us
    dot_general x1, matrix products, backward_of(): jnp.einsum('hts,thd->shd', grad_scores, query, preferred_element_type=jnp...  11.2 us
    dot_general x1, matrix products, backward_of(): jnp.einsum('hts,shd->thd', grad_scores, keys, preferred_element_type=jnp....  11.1 us
  transfers between devices with their start and end apart: 8, of which 7 were waited for; matrix products, arithmetic and copies ran while one was open for 6% of the time, Pallas kernels for 0%

commit v1 on v0

v1 whole, which is shorter than its diff:
```python
import jax
import jax.numpy as jnp
from jax import lax
from jax.experimental import pallas as pl
from jax.experimental.pallas import tpu as pltpu
from jax.sharding import PartitionSpec as P

GROUPS = 4
LANES = 4
BLOCK = 128


def visible_in(start, low, width, count):
    keys = lax.broadcasted_iota(jnp.int32, (count, width), 0)
    queries = lax.broadcasted_iota(jnp.int32, (count, width), 1) + low
    return (keys <= queries) & (keys >= start)


def probabilities(query, keys, start, low, scale):
    scores = lax.dot_general(
        keys, query, (((1,), (1,)), ((), ())), preferred_element_type=jnp.float32
    )
    scores = jnp.where(
        visible_in(start, low, query.shape[0], keys.shape[0]), scores * scale, -jnp.inf
    )
    top = jnp.max(scores, axis=0, keepdims=True)
    expo = jnp.exp(scores - top)
    return expo * (1.0 / jnp.sum(expo, axis=0, keepdims=True))


def document_starts(pos_ref, which):
    pos = pos_ref[pl.ds(which, 1), :]
    return lax.broadcasted_iota(jnp.int32, pos.shape, 1) - pos


def forward_kernel(which_ref, pos_ref, packed_ref, out_ref):
    heads, count, width = packed_ref.shape[0], packed_ref.shape[1], packed_ref.shape[2] // 3
    starts = document_starts(pos_ref, which_ref[0])
    for head in range(heads):
        values_t = packed_ref[head, :, 2 * width :].T
        for low in range(0, count, BLOCK):
            high = low + BLOCK
            probs = probabilities(
                packed_ref[head, low:high, :width],
                packed_ref[head, :high, width : 2 * width],
                starts[:, low:high],
                low,
                width**-0.5,
            )
            result = jnp.dot(
                values_t[:, :high], probs.astype(jnp.bfloat16), preferred_element_type=jnp.float32
            )
            out_ref[head, low:high, :] = result.T.astype(jnp.bfloat16)


def backward_kernel(
    which_ref, place_ref, pos_ref, grad_ref, early_ref, late_ref, out_ref, rows_ref, dk_ref, dv_ref
):
    heads, count, width = grad_ref.shape
    scale = width**-0.5
    starts = document_starts(pos_ref, which_ref[0])
    group, lane = place_ref[0], place_ref[1]
    piece = count // (GROUPS * LANES)
    for head in range(heads):
        for far in range(GROUPS):
            for side in range(LANES):
                source = lax.rem(group - far + GROUPS, GROUPS) * LANES + lax.rem(
                    lane - side + LANES, LANES
                )
                held = early_ref if far % 2 == 0 else late_ref
                rows_ref[pl.ds(pl.multiple_of(source * piece, 8), piece), :] = held[
                    far // 2, side, head
                ].astype(jnp.float32)
        keys_t = rows_ref[:, width : 2 * width].astype(jnp.bfloat16).T
        for low in range(0, count, BLOCK):
            high = low + BLOCK
            query = rows_ref[low:high, :width].astype(jnp.bfloat16)
            keys = rows_ref[:high, width : 2 * width].astype(jnp.bfloat16)
            values = rows_ref[:high, 2 * width :].astype(jnp.bfloat16)
            grad = grad_ref[head, low:high, :]
            probs = probabilities(query, keys, starts[:, low:high], low, scale)
            grad_probs = lax.dot_general(
                values, grad, (((1,), (1,)), ((), ())), preferred_element_type=jnp.float32
            )
            delta = jnp.sum(probs * grad_probs, axis=0, keepdims=True)
            grad_scores = (probs * (grad_probs - delta) * scale).astype(jnp.bfloat16)
            grad_values = jnp.dot(
                probs.astype(jnp.bfloat16), grad, preferred_element_type=jnp.float32
            )
            grad_keys = jnp.dot(grad_scores, query, preferred_element_type=jnp.float32)
            grad_query = jnp.dot(keys_t[:, :high], grad_scores, preferred_element_type=jnp.float32)
            out_ref[head, low:high, :width] = grad_query.T.astype(jnp.bfloat16)
            if low > 0:
                dv_ref[:low, :] += grad_values[:low]
                dk_ref[:low, :] += grad_keys[:low]
            dv_ref[low:high, :] = grad_values[low:]
            dk_ref[low:high, :] = grad_keys[low:]
        out_ref[head, :, width : 2 * width] = dk_ref[...].astype(jnp.bfloat16)
        out_ref[head, :, 2 * width :] = dv_ref[...].astype(jnp.bfloat16)


SCALARS = pl.BlockSpec(memory_space=pltpu.SMEM)
ARRAY = pl.BlockSpec(memory_space=pltpu.VMEM)
LIMIT = pltpu.CompilerParams(vmem_limit_bytes=32 * 1024 * 1024)


def forward_of(which, positions, packed):
    heads, count, width = packed.shape[0], packed.shape[1], packed.shape[2] // 3
    return pl.pallas_call(
        forward_kernel,
        out_shape=jax.ShapeDtypeStruct((heads, count, width), jnp.bfloat16),
        in_specs=[SCALARS, ARRAY, ARRAY],
        out_specs=ARRAY,
        compiler_params=LIMIT,
        name="forward_attention",
    )(which, positions, packed)


def backward_of(which, place, positions, grad_out, early, late):
    heads, count, width = grad_out.shape
    return pl.pallas_call(
        backward_kernel,
        out_shape=jax.ShapeDtypeStruct((heads, count, 3 * width), jnp.bfloat16),
        in_specs=[SCALARS, SCALARS] + [ARRAY] * 4,
        out_specs=ARRAY,
        scratch_shapes=[
            pltpu.VMEM((count, 3 * width), jnp.float32),
            pltpu.VMEM((count, width), jnp.float32),
            pltpu.VMEM((count, width), jnp.float32),
        ],
        compiler_params=LIMIT,
        name="backward_attention",
    )(which, place, positions, grad_out, early, late)


def passed_along(block, distance):
    count = lax.axis_size("pipe")
    route = [(i, i + distance) for i in range(count) if 0 <= i + distance < count]
    return lax.ppermute(block, "pipe", route)


def to_mirror(block, far):
    sections, size = lax.axis_size("pipe"), lax.axis_size("tensor")
    route = [
        (p * size + t, (sections - 2 - p) * size + (t + far * LANES) % size)
        for p in range(sections - 1)
        for t in range(size)
    ]
    return lax.ppermute(block, ("pipe", "tensor"), route)


def across_lanes(blocks):
    size = lax.axis_size("tensor")
    moved = [blocks[:, 0]]
    for side in range(1, LANES):
        route = [(t, t // LANES * LANES + (t + side) % LANES) for t in range(size)]
        moved.append(lax.ppermute(blocks[:, side], "tensor", route))
    return jnp.stack(moved, axis=1)


def local(fwd_qkv, held_stash, d_out, positions, plan):
    me = lax.axis_index("tensor")
    group, lane = me // LANES, me % LANES
    rows, heads, width = held_stash.shape[1:]
    mine = heads // (GROUPS * LANES)
    pieces = held_stash[0].transpose(1, 0, 2).reshape(GROUPS, LANES, mine, rows, width)
    pieces = jnp.roll(jnp.roll(pieces, -group, 0), -lane, 1)

    first = jnp.stack([to_mirror(pieces[0], 0), to_mirror(pieces[2], 2)])
    crossed = across_lanes(jnp.stack([pieces[1], pieces[3]]))
    late = jnp.stack([to_mirror(crossed[0], 1), to_mirror(crossed[1], 3)])
    early = across_lanes(first)

    attn_out = forward_of(plan[0, :1], positions, fwd_qkv[0].transpose(1, 0, 2))
    to_next = passed_along(attn_out, 1).transpose(1, 0, 2)

    grad_out = passed_along(d_out[0].transpose(1, 0, 2), -1)
    which = passed_along(plan, -1)
    place = jnp.stack([group, lane]).astype(jnp.int32)
    grads = backward_of(which[0, 1:], place, positions, grad_out, early, late)
    return to_next[None], grads.transpose(1, 0, 2)[None]


def solution(mesh):
    placed = (
        P("pipe", None, "tensor", None),
        P("pipe", "tensor", None, None),
        P("pipe", None, "tensor", None),
        P(),
        P("pipe", None),
    )
    return jax.shard_map(
        local,
        mesh=mesh,
        in_specs=placed,
        out_specs=(P("pipe", None, "tensor", None), P("pipe", None, "tensor", None)),
        check_vma=False,
    )
```

time: 322 us -> 124 us (0.39)
  the two profiles are of different devices: /device:TPU:36 before, /device:TPU:66 now
where the time goes in v1:
time: 124 us
  starting transfers between devices  79.1 us (64%)
  waiting for transfers between devices  23.8 us (19%)
  Pallas kernels  11.2 us (9%)
  local copies, waits for them, and re-layouts  6.76 us (5%)
  other arithmetic  1.63 us (1%)
    ppermute x4, starting transfers between devices, to_mirror(): return lax.ppermute(block, ('pipe', 'tensor'), route)  39.7 us
    ppermute x6, starting transfers between devices, across_lanes(): moved.append(lax.ppermute(blocks[:, side], 'tensor', route))  28.9 us
    ppermute x3, waiting for transfers between devices, passed_along(): return lax.ppermute(block, 'pipe', route)  16.8 us
    ppermute x3, starting transfers between devices, passed_along(): return lax.ppermute(block, 'pipe', route)  10.5 us
    pallas_call x1, Pallas kernels, backward_of(): pl.pallas_call(backward_kernel, out_shape=jax.ShapeDtypeStruct((heads, co...  8.31 us
    unnamed x14, local copies, waits for them, and re-layouts  5.84 us
    ppermute x6, waiting for transfers between devices, across_lanes(): moved.append(lax.ppermute(blocks[:, side], 'tensor', route))  3.73 us
    ppermute x4, waiting for transfers between devices, to_mirror(): return lax.ppermute(block, ('pipe', 'tensor'), route)  3.35 us
  transfers between devices with their start and end apart: 13, of which 4 were waited for; matrix products, arithmetic and copies ran while one was open for 2% of the time, Pallas kernels for 2%

profile of v1, /device:TPU:66, one launch (start us, length us, event | category | flops | bytes accessed | tf_op | source)
XLA Modules:
  0.0 123.6 jit_solution(17201139252447338708)
XLA Ops:
  0.7 1.8 %copy.21 = bf16[1,56,32,384]{3,1,2,0:T(8,128)(2,1)S(1)} copy(bf16[1,56,32,384]{3,2,1,0:T(8,128)(2,1)} %param.6) | data formatting | bytes 2752512 | tf_op args[1]
  2.5 0.6 fusion.1
  3.1 0.6 fusion
  3.7 0.1 slice_bitcast_fusion.5
  3.8 4.5 %collective-permute-start.3 = (bf16[4,2,56,384]{3,2,1,0:T(8,128)(2,1)S(1)}, bf16[4,2,56,384]{3,2,1,0:T(8,128)(2,1)S(1)}, u32[]{:S(2)}, u32[]{:S(2)}) collective-permute-start(bf16[4,2,56,384]{3,2,1,0:T(8,128)(2,1)S(1)} %get-tuple-element.6), channel_id=1, source_target_pairs={{0,480},{1,481},{2,482},{3,483},{4,484},{5,485},{6,486},{7,487},{8... | collective-permute-start | bytes 1032200 | tf_op jit(solution)/shard_map/ppermute | solution.py:149
  8.2 0.0 copy-start.2
  8.3 14.2 %collective-permute-start.4 = (bf16[4,2,56,384]{3,2,1,0:T(8,128)(2,1)S(1)}, bf16[4,2,56,384]{3,2,1,0:T(8,128)(2,1)S(1)}, u32[]{:S(2)}, u32[]{:S(2)}) collective-permute-start(bf16[4,2,56,384]{3,2,1,0:T(8,128)(2,1)S(1)} %get-tuple-element.7), channel_id=1, source_target_pairs={{0,488},{1,489},{2,490},{3,491},{4,492},{5,493},{6,494},{7,495},{8... | collective-permute-start | bytes 1032200 | tf_op jit(solution)/shard_map/ppermute | solution.py:149
  22.5 0.1 fusion.2
  22.5 0.1 slice_bitcast_fusion.9
  22.6 3.4 %collective-permute-start.8 = (bf16[2,2,56,384]{3,2,1,0:T(8,128)(2,1)S(1)}, bf16[2,2,56,384]{3,2,1,0:T(8,128)(2,1)S(1)}, u32[]{:S(2)}, u32[]{:S(2)}) collective-permute-start(bf16[2,2,56,384]{3,2,1,0:T(8,128)(2,1)S(1)} %get-tuple-element.13), channel_id=1, source_target_pairs={{0,1},{1,2},{2,3},{3,0},{4,5},{5,6},{6,7},{7,4},{8,9},{9,10},{10,1... | collective-permute-start | bytes 516104 | tf_op jit(solution)/shard_map/ppermute | solution.py:157
  26.0 3.0 %collective-permute-start.9 = (bf16[2,2,56,384]{3,2,1,0:T(8,128)(2,1)S(1)}, bf16[2,2,56,384]{3,2,1,0:T(8,128)(2,1)S(1)}, u32[]{:S(2)}, u32[]{:S(2)}) collective-permute-start(bf16[2,2,56,384]{3,2,1,0:T(8,128)(2,1)S(1)} %get-tuple-element.12), channel_id=1, source_target_pairs={{0,2},{1,3},{2,0},{3,1},{4,6},{5,7},{6,4},{7,5},{8,10},{9,11},{10,... | collective-permute-start | bytes 516104 | tf_op jit(solution)/shard_map/ppermute | solution.py:157
  29.1 0.0 copy-start
  29.1 0.0 copy-start.1
  29.1 4.1 %collective-permute-start.10 = (bf16[2,2,56,384]{3,2,1,0:T(8,128)(2,1)S(1)}, bf16[2,2,56,384]{3,2,1,0:T(8,128)(2,1)S(1)}, u32[]{:S(2)}, u32[]{:S(2)}) collective-permute-start(bf16[2,2,56,384]{3,2,1,0:T(8,128)(2,1)S(1)} %get-tuple-element.11), channel_id=1, source_target_pairs={{0,3},{1,0},{2,1},{3,2},{4,7},{5,4},{6,5},{7,6},{8,11},{9,8},{10,9... | collective-permute-start | bytes 516104 | tf_op jit(solution)/shard_map/ppermute | solution.py:157
  33.2 0.0 copy-done.2
  33.2 0.2 copy.48
  33.3 0.0 copy-done
  33.4 0.0 copy-done.1
  33.4 2.9 %forward_attention.1 = bf16[2,896,128]{2,1,0:T(8,128)(2,1)S(1)} custom-call(s32[1]{0:T(128)S(1)} %bitcast.84, s32[4,896]{1,0:T(4,128)S(1)} %copy-done, bf16[2,896,384]{2,1,0:T(8,128)(2,1)S(1)} %bitcast.83), custom_call_target="tpu_custom_call" | custom-call | tf_op jit(solution)/shard_map/forward_attention/pallas_call | solution.py:109
  36.3 0.0 collective-permute-done.8
  36.3 1.9 %collective-permute-start = (bf16[2,896,128]{2,1,0:T(8,128)(2,1)S(1)}, bf16[2,896,128]{2,1,0:T(8,128)(2,1)S(1)}, u32[]{:S(2)}, u32[]{:S(2)}) collective-permute-start(bf16[2,896,128]{2,1,0:T(8,128)(2,1)S(1)} %forward_attention.1), channel_id=1, source_target_pairs={{0,16},{16,32},{32,48},{48,64},{64,80},{80,96},{96,112},{112,128},... | collective-permute-start | bytes 1376264 | tf_op jit(solution)/shard_map/ppermute | solution.py:139
  38.2 0.0 collective-permute-done.9
  38.3 0.4 collective-permute-done.10
  38.7 0.1 pad_maximum_fusion.1
  38.8 0.0 collective-permute-done.3
  38.8 3.3 %collective-permute-done.4 = bf16[4,2,56,384]{3,2,1,0:T(8,128)(2,1)S(1)} collective-permute-done((bf16[4,2,56,384]{3,2,1,0:T(8,128)(2,1)S(1)}, bf16[4,2,56,384]{3,2,1,0:T(8,128)(2,1)S(1)}, u32[]{:S(2)}, u32[]{:S(2)}) %collective-permute-start.4) | collective-permute-done | bytes 344096 | tf_op jit(solution)/shard_map/ppermute | solution.py:149
  42.1 0.0 copy-start.3
  42.1 0.1 fusion.7
  42.2 3.5 %collective-permute-start.5 = (bf16[2,2,56,384]{3,2,1,0:T(8,128)(2,1)S(1)}, bf16[2,2,56,384]{3,2,1,0:T(8,128)(2,1)S(1)}, u32[]{:S(2)}, u32[]{:S(2)}) collective-permute-start(bf16[2,2,56,384]{3,2,1,0:T(8,128)(2,1)S(1)} %get-tuple-element.15), channel_id=1, source_target_pairs={{0,1},{1,2},{2,3},{3,0},{4,5},{5,6},{6,7},{7,4},{8,9},{9,10},{10,1... | collective-permute-start | bytes 516104 | tf_op jit(solution)/shard_map/ppermute | solution.py:157
  45.8 0.1 slice_bitcast_fusion.1
  45.9 16.5 %collective-permute-start.11 = (bf16[4,2,56,384]{3,2,1,0:T(8,128)(2,1)S(1)}, bf16[4,2,56,384]{3,2,1,0:T(8,128)(2,1)S(1)}, u32[]{:S(2)}, u32[]{:S(2)}) collective-permute-start(bf16[4,2,56,384]{3,2,1,0:T(8,128)(2,1)S(1)} %get-tuple-element.8), channel_id=1, source_target_pairs={{0,484},{1,485},{2,486},{3,487},{4,488},{5,489},{6,490},{7,491},{8... | collective-permute-start | bytes 1032200 | tf_op jit(solution)/shard_map/ppermute | solution.py:149
  62.4 4.5 %collective-permute-start.12 = (bf16[4,2,56,384]{3,2,1,0:T(8,128)(2,1)S(1)}, bf16[4,2,56,384]{3,2,1,0:T(8,128)(2,1)S(1)}, u32[]{:S(2)}, u32[]{:S(2)}) collective-permute-start(bf16[4,2,56,384]{3,2,1,0:T(8,128)(2,1)S(1)} %get-tuple-element.9), channel_id=1, source_target_pairs={{0,492},{1,493},{2,494},{3,495},{4,480},{5,481},{6,482},{7,483},{8... | collective-permute-start | bytes 1032200 | tf_op jit(solution)/shard_map/ppermute | solution.py:149
  66.9 1.9 %collective-permute-start.1 = (s32[1,2]{1,0:T(1,128)S(1)}, s32[1,2]{1,0:T(1,128)S(1)}, u32[]{:S(2)}, u32[]{:S(2)}) collective-permute-start(s32[1,2]{1,0:T(1,128)S(1)} %copy-done.1), channel_id=1, source_target_pairs={{16,0},{32,16},{48,32},{64,48},{80,64},{96,80},{112,96},{128,112},... | collective-permute-start | bytes 32 | tf_op jit(solution)/shard_map/ppermute | solution.py:139
  68.9 0.0 copy-done.3
  68.9 0.1 copy.49
  68.9 16.8 %collective-permute-done.1 = s32[1,2]{1,0:T(1,128)S(1)} collective-permute-done((s32[1,2]{1,0:T(1,128)S(1)}, s32[1,2]{1,0:T(1,128)S(1)}, u32[]{:S(2)}, u32[]{:S(2)}) %collective-permute-start.1) | collective-permute-done | bytes 40 | tf_op jit(solution)/shard_map/ppermute | solution.py:139
  85.7 6.7 %collective-permute-start.2 = (bf16[2,896,128]{2,1,0:T(8,128)(2,1)S(1)}, bf16[2,896,128]{2,1,0:T(8,128)(2,1)S(1)}, u32[]{:S(2)}, u32[]{:S(2)}) collective-permute-start(bf16[2,896,128]{2,1,0:T(8,128)(2,1)S(1)} %bitcast.87), channel_id=1, source_target_pairs={{16,0},{32,16},{48,32},{64,48},{80,64},{96,80},{112,96},{128,112},... | collective-permute-start | bytes 1376264 | tf_op jit(solution)/shard_map/ppermute | solution.py:139
  92.4 0.0 collective-permute-done
  92.4 12.8 %collective-permute-start.6 = (bf16[2,2,56,384]{3,2,1,0:T(8,128)(2,1)S(1)}, bf16[2,2,56,384]{3,2,1,0:T(8,128)(2,1)S(1)}, u32[]{:S(2)}, u32[]{:S(2)}) collective-permute-start(bf16[2,2,56,384]{3,2,1,0:T(8,128)(2,1)S(1)} %get-tuple-element.17), channel_id=1, source_target_pairs={{0,2},{1,3},{2,0},{3,1},{4,6},{5,7},{6,4},{7,5},{8,10},{9,11},{10,... | collective-permute-start | bytes 516104 | tf_op jit(solution)/shard_map/ppermute | solution.py:157
  105.1 0.0 collective-permute-done.5
  105.1 2.1 %collective-permute-start.7 = (bf16[2,2,56,384]{3,2,1,0:T(8,128)(2,1)S(1)}, bf16[2,2,56,384]{3,2,1,0:T(8,128)(2,1)S(1)}, u32[]{:S(2)}, u32[]{:S(2)}) collective-permute-start(bf16[2,2,56,384]{3,2,1,0:T(8,128)(2,1)S(1)} %get-tuple-element.16), channel_id=1, source_target_pairs={{0,3},{1,0},{2,1},{3,2},{4,7},{5,4},{6,5},{7,6},{8,11},{9,8},{10,9... | collective-permute-start | bytes 516104 | tf_op jit(solution)/shard_map/ppermute | solution.py:157
  107.3 0.1 pad_add_fusion.place_ref
  107.3 0.6 slice.49
  107.9 1.2 %copy.32 = bf16[1,896,2,128]{3,2,1,0:T(2,128)(2,1)} copy(bf16[1,896,2,128]{3,1,2,0:T(8,128)(2,1)S(1)} %bitcast.86) | data formatting | bytes 917504
  109.2 0.0 collective-permute-done.6
  109.2 3.3 %collective-permute-done.7 = bf16[2,2,56,384]{3,2,1,0:T(8,128)(2,1)S(1)} collective-permute-done((bf16[2,2,56,384]{3,2,1,0:T(8,128)(2,1)S(1)}, bf16[2,2,56,384]{3,2,1,0:T(8,128)(2,1)S(1)}, u32[]{:S(2)}, u32[]{:S(2)}) %collective-permute-start.7) | collective-permute-done | bytes 172064 | tf_op jit(solution)/shard_map/ppermute | solution.py:157
  112.4 0.1 pad_maximum_fusion
  112.6 0.1 copy.31.early_ref
  112.6 0.0 collective-permute-done.11
  112.6 0.0 collective-permute-done.12
  112.7 0.1 pad_maximum_fusion.2.late_ref
  112.7 0.0 collective-permute-done.2.grad_ref
  112.8 8.3 %backward_attention.1 = bf16[2,896,384]{2,1,0:T(8,128)(2,1)S(1)} custom-call(s32[1]{0:T(128)} %bitcast.5.which_ref, s32[2]{0:T(128)S(1)} %pad_add_fusion.place_ref, s32[4,896]{1,0:T(4,128)S(1)} %copy-done, bf16[2,896,128]{2,1,0:T(8,128)(2,1)S(1)} %collective-permute-done.2.grad_ref, bf16[2,4,2,56,384]{4,3,2,1,0:T(8,128)(2,1)S(1)} %copy.31.early_ref, ...), custom_call_target="tpu_custom_call" | custom-call | tf_op jit(solution)/shard_map/backward_attention/pallas_call | solution.py:121
  121.1 2.5 %copy.33 = bf16[1,896,2,384]{3,2,1,0:T(2,128)(2,1)} copy(bf16[1,896,2,384]{3,1,2,0:T(8,128)(2,1)S(1)} %bitcast.82) | data formatting | bytes 2752512
  (1 shorter events, 0.0 us)
Async XLA Ops:
  3.8 35.0 %collective-permute-start.3 = (bf16[4,2,56,384]{3,2,1,0:T(8,128)(2,1)S(1)}, bf16[4,2,56,384]{3,2,1,0:T(8,128)(2,1)S(1)}, u32[]{:S(2)}, u32[]{:S(2)}) collective-permute-start(bf16[4,2,56,384]{3,2,1,0:T(8,128)(2,1)S(1)} %get-tuple-element.6), channel_id=1, source_target_pairs={{0,480},{1,481},{2,482},{3,483},{4,484},{5,485},{6,486},{7,487},{8... | collective-permute-start | bytes 1032200 | tf_op jit(solution)/shard_map/ppermute | solution.py:149
  8.2 24.9 %copy-start.2 = (bf16[1,896,2,384]{3,2,1,0:T(2,128)(2,1)S(1)}, bf16[1,896,2,384]{3,2,1,0:T(2,128)(2,1)}, u32[]{:S(2)}) copy-start(bf16[1,896,2,384]{3,2,1,0:T(2,128)(2,1)} %param.5) | copy-start | bytes 4128772
  8.3 33.9 %collective-permute-start.4 = (bf16[4,2,56,384]{3,2,1,0:T(8,128)(2,1)S(1)}, bf16[4,2,56,384]{3,2,1,0:T(8,128)(2,1)S(1)}, u32[]{:S(2)}, u32[]{:S(2)}) collective-permute-start(bf16[4,2,56,384]{3,2,1,0:T(8,128)(2,1)S(1)} %get-tuple-element.7), channel_id=1, source_target_pairs={{0,488},{1,489},{2,490},{3,491},{4,492},{5,493},{6,494},{7,495},{8... | collective-permute-start | bytes 1032200 | tf_op jit(solution)/shard_map/ppermute | solution.py:149
  22.6 13.7 %collective-permute-start.8 = (bf16[2,2,56,384]{3,2,1,0:T(8,128)(2,1)S(1)}, bf16[2,2,56,384]{3,2,1,0:T(8,128)(2,1)S(1)}, u32[]{:S(2)}, u32[]{:S(2)}) collective-permute-start(bf16[2,2,56,384]{3,2,1,0:T(8,128)(2,1)S(1)} %get-tuple-element.13), channel_id=1, source_target_pairs={{0,1},{1,2},{2,3},{3,0},{4,5},{5,6},{6,7},{7,4},{8,9},{9,10},{10,1... | collective-permute-start | bytes 516104 | tf_op jit(solution)/shard_map/ppermute | solution.py:157
  26.0 12.2 %collective-permute-start.9 = (bf16[2,2,56,384]{3,2,1,0:T(8,128)(2,1)S(1)}, bf16[2,2,56,384]{3,2,1,0:T(8,128)(2,1)S(1)}, u32[]{:S(2)}, u32[]{:S(2)}) collective-permute-start(bf16[2,2,56,384]{3,2,1,0:T(8,128)(2,1)S(1)} %get-tuple-element.12), channel_id=1, source_target_pairs={{0,2},{1,3},{2,0},{3,1},{4,6},{5,7},{6,4},{7,5},{8,10},{9,11},{10,... | collective-permute-start | bytes 516104 | tf_op jit(solution)/shard_map/ppermute | solution.py:157
  29.1 4.3 %copy-start = (s32[4,896]{1,0:T(4,128)S(1)}, s32[4,896]{1,0:T(4,128)}, u32[]{:S(2)}) copy-start(s32[4,896]{1,0:T(4,128)} %pos_ref.3) | copy-start | bytes 43012
  29.1 4.3 %copy-start.1 = (s32[1,2]{1,0:T(1,128)S(1)}, s32[1,2]{1,0:T(1,128)}, u32[]{:S(2)}) copy-start(s32[1,2]{1,0:T(1,128)} %param.9) | copy-start | bytes 28
  29.1 9.6 %collective-permute-start.10 = (bf16[2,2,56,384]{3,2,1,0:T(8,128)(2,1)S(1)}, bf16[2,2,56,384]{3,2,1,0:T(8,128)(2,1)S(1)}, u32[]{:S(2)}, u32[]{:S(2)}) collective-permute-start(bf16[2,2,56,384]{3,2,1,0:T(8,128)(2,1)S(1)} %get-tuple-element.11), channel_id=1, source_target_pairs={{0,3},{1,0},{2,1},{3,2},{4,7},{5,4},{6,5},{7,6},{8,11},{9,8},{10,9... | collective-permute-start | bytes 516104 | tf_op jit(solution)/shard_map/ppermute | solution.py:157
  36.3 56.0 %collective-permute-start = (bf16[2,896,128]{2,1,0:T(8,128)(2,1)S(1)}, bf16[2,896,128]{2,1,0:T(8,128)(2,1)S(1)}, u32[]{:S(2)}, u32[]{:S(2)}) collective-permute-start(bf16[2,896,128]{2,1,0:T(8,128)(2,1)S(1)} %forward_attention.1), channel_id=1, source_target_pairs={{0,16},{16,32},{32,48},{48,64},{64,80},{80,96},{96,112},{112,128},... | collective-permute-start | bytes 1376264 | tf_op jit(solution)/shard_map/ppermute | solution.py:139
  42.1 26.7 %copy-start.3 = (bf16[1,896,2,128]{3,2,1,0:T(2,128)(2,1)S(1)}, bf16[1,896,2,128]{3,2,1,0:T(2,128)(2,1)}, u32[]{:S(2)}) copy-start(bf16[1,896,2,128]{3,2,1,0:T(2,128)(2,1)} %param.7) | copy-start | bytes 1376260
  42.2 62.9 %collective-permute-start.5 = (bf16[2,2,56,384]{3,2,1,0:T(8,128)(2,1)S(1)}, bf16[2,2,56,384]{3,2,1,0:T(8,128)(2,1)S(1)}, u32[]{:S(2)}, u32[]{:S(2)}) collective-permute-start(bf16[2,2,56,384]{3,2,1,0:T(8,128)(2,1)S(1)} %get-tuple-element.15), channel_id=1, source_target_pairs={{0,1},{1,2},{2,3},{3,0},{4,5},{5,6},{6,7},{7,4},{8,9},{9,10},{10,1... | collective-permute-start | bytes 516104 | tf_op jit(solution)/shard_map/ppermute | solution.py:157
  45.9 66.8 %collective-permute-start.11 = (bf16[4,2,56,384]{3,2,1,0:T(8,128)(2,1)S(1)}, bf16[4,2,56,384]{3,2,1,0:T(8,128)(2,1)S(1)}, u32[]{:S(2)}, u32[]{:S(2)}) collective-permute-start(bf16[4,2,56,384]{3,2,1,0:T(8,128)(2,1)S(1)} %get-tuple-element.8), channel_id=1, source_target_pairs={{0,484},{1,485},{2,486},{3,487},{4,488},{5,489},{6,490},{7,491},{8... | collective-permute-start | bytes 1032200 | tf_op jit(solution)/shard_map/ppermute | solution.py:149
  62.4 50.3 %collective-permute-start.12 = (bf16[4,2,56,384]{3,2,1,0:T(8,128)(2,1)S(1)}, bf16[4,2,56,384]{3,2,1,0:T(8,128)(2,1)S(1)}, u32[]{:S(2)}, u32[]{:S(2)}) collective-permute-start(bf16[4,2,56,384]{3,2,1,0:T(8,128)(2,1)S(1)} %get-tuple-element.9), channel_id=1, source_target_pairs={{0,492},{1,493},{2,494},{3,495},{4,480},{5,481},{6,482},{7,483},{8... | collective-permute-start | bytes 1032200 | tf_op jit(solution)/shard_map/ppermute | solution.py:149
  66.9 18.8 %collective-permute-start.1 = (s32[1,2]{1,0:T(1,128)S(1)}, s32[1,2]{1,0:T(1,128)S(1)}, u32[]{:S(2)}, u32[]{:S(2)}) collective-permute-start(s32[1,2]{1,0:T(1,128)S(1)} %copy-done.1), channel_id=1, source_target_pairs={{16,0},{32,16},{48,32},{64,48},{80,64},{96,80},{112,96},{128,112},... | collective-permute-start | bytes 32 | tf_op jit(solution)/shard_map/ppermute | solution.py:139
  85.7 27.1 %collective-permute-start.2 = (bf16[2,896,128]{2,1,0:T(8,128)(2,1)S(1)}, bf16[2,896,128]{2,1,0:T(8,128)(2,1)S(1)}, u32[]{:S(2)}, u32[]{:S(2)}) collective-permute-start(bf16[2,896,128]{2,1,0:T(8,128)(2,1)S(1)} %bitcast.87), channel_id=1, source_target_pairs={{16,0},{32,16},{48,32},{64,48},{80,64},{96,80},{112,96},{128,112},... | collective-permute-start | bytes 1376264 | tf_op jit(solution)/shard_map/ppermute | solution.py:139
  92.4 16.8 %collective-permute-start.6 = (bf16[2,2,56,384]{3,2,1,0:T(8,128)(2,1)S(1)}, bf16[2,2,56,384]{3,2,1,0:T(8,128)(2,1)S(1)}, u32[]{:S(2)}, u32[]{:S(2)}) collective-permute-start(bf16[2,2,56,384]{3,2,1,0:T(8,128)(2,1)S(1)} %get-tuple-element.17), channel_id=1, source_target_pairs={{0,2},{1,3},{2,0},{3,1},{4,6},{5,7},{6,4},{7,5},{8,10},{9,11},{10,... | collective-permute-start | bytes 516104 | tf_op jit(solution)/shard_map/ppermute | solution.py:157
  105.1 7.3 %collective-permute-start.7 = (bf16[2,2,56,384]{3,2,1,0:T(8,128)(2,1)S(1)}, bf16[2,2,56,384]{3,2,1,0:T(8,128)(2,1)S(1)}, u32[]{:S(2)}, u32[]{:S(2)}) collective-permute-start(bf16[2,2,56,384]{3,2,1,0:T(8,128)(2,1)S(1)} %get-tuple-element.16), channel_id=1, source_target_pairs={{0,3},{1,0},{2,1},{3,2},{4,7},{5,4},{6,5},{7,6},{8,11},{9,8},{10,9... | collective-permute-start | bytes 516104 | tf_op jit(solution)/shard_map/ppermute | solution.py:157

commit v2 on v1

v2 whole, which is shorter than its diff:
```python
import functools

import jax
import jax.numpy as jnp
from jax import lax
from jax.experimental import pallas as pl
from jax.experimental.pallas import tpu as pltpu
from jax.sharding import PartitionSpec as P

GROUPS = 4
LANES = 4
BLOCK = 128
FLOPS = 50_000_000_000
FIRST = (0, 2, )
LATE = (1, 3, )


def visible_in(start, low, width, count):
    keys = lax.broadcasted_iota(jnp.int32, (count, width), 0)
    queries = lax.broadcasted_iota(jnp.int32, (count, width), 1) + low
    return (keys <= queries) & (keys >= start)


def probabilities(query, keys, start, low, scale):
    scores = lax.dot_general(
        keys, query, (((1,), (1,)), ((), ())), preferred_element_type=jnp.float32
    )
    scores = jnp.where(
        visible_in(start, low, query.shape[0], keys.shape[0]), scores * scale, -jnp.inf
    )
    top = jnp.max(scores, axis=0, keepdims=True)
    expo = jnp.exp(scores - top)
    return expo * (1.0 / jnp.sum(expo, axis=0, keepdims=True))


def document_starts(pos_ref, which, low, width):
    starts = jnp.zeros((1, width), jnp.int32)
    for batch in range(pos_ref.shape[0]):
        starts = jnp.where(which == batch, pos_ref[batch : batch + 1, low : low + width], starts)
    return lax.broadcasted_iota(jnp.int32, starts.shape, 1) + low - starts


def forward_kernel(head, which_ref, pos_ref, packed_ref, out_ref):
    count, width = packed_ref.shape[1], packed_ref.shape[2] // 3
    values_t = packed_ref[head, :, 2 * width :].T
    for low in range(0, count, BLOCK):
        high = low + BLOCK
        probs = probabilities(
            packed_ref[head, low:high, :width],
            packed_ref[head, :high, width : 2 * width],
            document_starts(pos_ref, which_ref[0, 0], low, BLOCK),
            low,
            width**-0.5,
        )
        result = jnp.dot(
            values_t[:, :high], probs.astype(jnp.bfloat16), preferred_element_type=jnp.float32
        )
        out_ref[low:high, :] = result.T.astype(jnp.bfloat16)


def backward_kernel(
    place_ref, pos_ref, grad_ref, early_ref, late_ref, out_ref, rows_ref, dk_ref, dv_ref
):
    heads, count, width = out_ref.shape[0], out_ref.shape[1], grad_ref.shape[2]
    scale = width**-0.5
    which = grad_ref[0, count : count + 1, :].astype(jnp.float32)
    group = place_ref[0]
    piece = count // (GROUPS * LANES)
    for head in range(heads):
        for far in range(GROUPS):
            for side in range(LANES):
                source = lax.rem(group - far + GROUPS, GROUPS) * LANES + side
                held, number = (early_ref, FIRST.index(far)) if far in FIRST else (late_ref, LATE.index(far))
                rows_ref[pl.ds(pl.multiple_of(source * piece, 8), piece), :] = held[
                    number, side, head
                ].astype(jnp.float32)
        keys_t = rows_ref[:, width : 2 * width].astype(jnp.bfloat16).T
        for low in range(0, count, BLOCK):
            high = low + BLOCK
            query = rows_ref[low:high, :width].astype(jnp.bfloat16)
            keys = rows_ref[:high, width : 2 * width].astype(jnp.bfloat16)
            values = rows_ref[:high, 2 * width :].astype(jnp.bfloat16)
            grad = grad_ref[head, low:high, :]
            starts = document_starts(pos_ref, which, low, BLOCK)
            probs = probabilities(query, keys, starts, low, scale)
            grad_probs = lax.dot_general(
                values, grad, (((1,), (1,)), ((), ())), preferred_element_type=jnp.float32
            )
            delta = jnp.sum(probs * grad_probs, axis=0, keepdims=True)
            grad_scores = (probs * (grad_probs - delta) * scale).astype(jnp.bfloat16)
            grad_values = jnp.dot(
                probs.astype(jnp.bfloat16), grad, preferred_element_type=jnp.float32
            )
            grad_keys = jnp.dot(grad_scores, query, preferred_element_type=jnp.float32)
            grad_query = jnp.dot(keys_t[:, :high], grad_scores, preferred_element_type=jnp.float32)
            out_ref[head, low:high, :width] = grad_query.T.astype(jnp.bfloat16)
            if low > 0:
                dv_ref[:low, :] += grad_values[:low]
                dk_ref[:low, :] += grad_keys[:low]
            dv_ref[low:high, :] = grad_values[low:]
            dk_ref[low:high, :] = grad_keys[low:]
        out_ref[head, :, width : 2 * width] = dk_ref[...].astype(jnp.bfloat16)
        out_ref[head, :, 2 * width :] = dv_ref[...].astype(jnp.bfloat16)


SCALARS = pl.BlockSpec(memory_space=pltpu.SMEM)
ARRAY = pl.BlockSpec(memory_space=pltpu.VMEM)
LIMIT = pltpu.CompilerParams(vmem_limit_bytes=32 * 1024 * 1024)


def forward_of(head, plan, positions, packed):
    count, width = packed.shape[1], packed.shape[2] // 3
    return pl.pallas_call(
        functools.partial(forward_kernel, head),
        out_shape=jax.ShapeDtypeStruct((count, width), jnp.bfloat16),
        in_specs=[SCALARS, ARRAY, ARRAY],
        out_specs=ARRAY,
        compiler_params=LIMIT,
        cost_estimate=pl.CostEstimate(flops=FLOPS, bytes_accessed=0, transcendentals=0),
        name="forward_attention",
    )(plan, positions, packed)


def backward_of(place, positions, grad_out, early, late):
    width = grad_out.shape[2]
    heads, count = early.shape[2], positions.shape[1]
    return pl.pallas_call(
        backward_kernel,
        out_shape=jax.ShapeDtypeStruct((heads, count, 3 * width), jnp.bfloat16),
        in_specs=[SCALARS] + [ARRAY] * 4,
        out_specs=ARRAY,
        scratch_shapes=[
            pltpu.VMEM((count, 3 * width), jnp.float32),
            pltpu.VMEM((count, width), jnp.float32),
            pltpu.VMEM((count, width), jnp.float32),
        ],
        compiler_params=LIMIT,
        name="backward_attention",
    )(place, positions, grad_out, early, late)


def stack_kernel(*refs):
    for number, ref in enumerate(refs[:-1]):
        refs[-1][number] = ref[...]


def stacked(pieces):
    return pl.pallas_call(
        stack_kernel,
        out_shape=jax.ShapeDtypeStruct((len(pieces), *pieces[0].shape), pieces[0].dtype),
        in_specs=[ARRAY] * len(pieces),
        out_specs=ARRAY,
        compiler_params=LIMIT,
        cost_estimate=pl.CostEstimate(flops=FLOPS, bytes_accessed=0, transcendentals=0),
        name="stacked",
    )(*pieces)


def passed_along(block, distance):
    count = lax.axis_size("pipe")
    route = [(i, i + distance) for i in range(count) if 0 <= i + distance < count]
    return lax.ppermute(block, "pipe", route)


def to_mirror(block, far):
    sections, size = lax.axis_size("pipe"), lax.axis_size("tensor")
    route = [
        (p * size + t, (sections - 2 - p) * size + (t + far * LANES) % size)
        for p in range(sections - 1)
        for t in range(size)
    ]
    return lax.ppermute(block, ("pipe", "tensor"), route)


def across_lanes(blocks):
    size = lax.axis_size("tensor")
    rows = [list(range(low, low + LANES)) for low in range(0, size, LANES)]
    return lax.all_to_all(
        blocks, "tensor", split_axis=1, concat_axis=1, axis_index_groups=rows, tiled=True
    )


def local(fwd_qkv, held_stash, d_out, positions, plan):
    me = lax.axis_index("tensor")
    group = me // LANES
    rows, heads, width = held_stash.shape[1:]
    mine = heads // (GROUPS * LANES)
    count = d_out.shape[1]

    def for_group(far):
        low = (group + far) % GROUPS * (LANES * mine)
        piece = lax.dynamic_slice_in_dim(held_stash[0], low, LANES * mine, 1)
        return piece.reshape(rows * LANES * mine, width)

    def by_lane(pieces):
        split = pieces.reshape(-1, rows, LANES, mine, width).transpose(0, 2, 3, 1, 4)
        return split

    def after(value, other):
        return lax.optimization_barrier((value, other))[0]

    first = stacked([to_mirror(for_group(far), far) for far in FIRST])
    crossed = across_lanes(by_lane(jnp.stack([for_group(far) for far in LATE])))
    late = stacked([to_mirror(crossed[n], far) for n, far in enumerate(LATE)])
    early = across_lanes(by_lane(first))
    packed = fwd_qkv[0].transpose(1, 0, 2)
    attn_out = jnp.stack([forward_of(head, plan, positions, packed) for head in range(mine)])
    which = jnp.broadcast_to(plan[0, 1].astype(jnp.bfloat16), (mine, 16, d_out.shape[3]))
    grad_out = passed_along(jnp.concatenate([after(d_out, attn_out)[0].transpose(1, 0, 2), which], axis=1), -1)
    to_next = passed_along(after(attn_out, grad_out), 1).transpose(1, 0, 2)
    place = group.astype(jnp.int32)[None]
    grads = backward_of(place, positions, grad_out, early, late)
    return to_next[None], grads.transpose(1, 0, 2)[None]


def solution(mesh):
    placed = (
        P("pipe", None, "tensor", None),
        P("pipe", "tensor", None, None),
        P("pipe", None, "tensor", None),
        P(),
        P("pipe", None),
    )
    return jax.shard_map(
        local,
        mesh=mesh,
        in_specs=placed,
        out_specs=(P("pipe", None, "tensor", None), P("pipe", None, "tensor", None)),
        check_vma=False,
    )
```

time: 124 us -> 103 us (0.83)
  the two profiles are of different devices: /device:TPU:66 before, /device:TPU:59 now
where the time goes in v2:
time: 103 us; the launch traced here: 102 us
  starting transfers between devices  42.3 us (41%)
  waiting for transfers between devices  35.8 us (35%)
  Pallas kernels  11.8 us (11%)
  local copies, waits for them, and re-layouts  10.4 us (10%)
    ppermute x2, waiting for transfers between devices, passed_along(): return lax.ppermute(block, 'pipe', route)  35.8 us
    ppermute x4, starting transfers between devices, to_mirror(): return lax.ppermute(block, ('pipe', 'tensor'), route)  25.3 us
    all_to_all x2, starting transfers between devices, across_lanes(): lax.all_to_all(blocks, 'tensor', split_axis=1, concat_axis=1, axis_index_...  8.5 us
    ppermute x2, starting transfers between devices, passed_along(): return lax.ppermute(block, 'pipe', route)  8.47 us
    pallas_call x1, Pallas kernels, backward_of(): pl.pallas_call(backward_kernel, out_shape=jax.ShapeDtypeStruct((heads, co...  7.1 us
    pallas_call x2, Pallas kernels, forward_of(): pl.pallas_call(functools.partial(forward_kernel, head), out_shape=jax.Sha...  4.58 us
    unnamed x11, local copies, waits for them, and re-layouts  3.94 us
    dynamic_slice x3, local copies, waits for them, and re-layouts, for_group(): piece = lax.dynamic_slice_in_dim(held_stash[0], low, LANES * mine, 1)  2.37 us
  transfers between devices with their start and end apart: 8, of which 1 were waited for; matrix products, arithmetic and copies ran while one was open for 7% of the time, Pallas kernels for 12%

profile of v2, /device:TPU:59, one launch (start us, length us, event | category | flops | bytes accessed | tf_op | source)
XLA Modules:
  0.0 102.3 jit_solution(14770672017396032508)
XLA Ops:
  0.7 2.3 %constant_dynamic-slice_fusion.1 = (bf16[1,56,8,384]{3,2,1,0:T(8,128)(2,1)S(1)}, bf16[448,384]{1,0:T(8,128)(2,1)}, bf16[448,384]{1,0:T(8,128)(2,1)}, bf16[1,56,8,384]{3,2,1,0:T(8,128)(2,1)S(1)}) fusion(bf16[1,56,32,384]{3,2,1,0:T(8,128)(2,1)} %param.6, s32[]{:T(128)S(6)} %select_n.41, s32[]{:T(128)S(6)} %select_n.39, s32[]{:T(128)S(6)} %select_n.37, ...), kind=kLoop, calls=%fused_computation.9 | loop fusion | bytes 2752528 | tf_op jit(solution)/shard_map/dynamic_slice | solution.py:192
  3.1 0.0 copy-start.2
  3.1 0.9 maximum_bitcast_fusion
  4.0 4.3 %all-to-all-start.1 = ((bf16[2,4,2,56,384]{4,3,2,0,1:T(8,128)(2,1)}), bf16[2,4,2,56,384]{4,3,2,0,1:T(8,128)(2,1)S(1)}, u32[]{:S(2)}, u32[]{:S(2)}) async-start(bf16[2,4,2,56,384]{4,3,2,0,1:T(8,128)(2,1)} %maximum_bitcast_fusion), calls=%async_computation.1 | async-start | bytes 1376256 | tf_op jit(solution)/shard_map/all_to_all | solution.py:178
  8.3 14.5 %collective-permute-start.3 = (bf16[448,384]{1,0:T(8,128)(2,1)}, bf16[448,384]{1,0:T(8,128)(2,1)S(1)}, u32[]{:S(2)}, u32[]{:S(2)}) collective-permute-start(bf16[448,384]{1,0:T(8,128)(2,1)} %get-tuple-element.13), channel_id=1, source_target_pairs={{0,488},{1,489},{2,490},{3,491},{4,492},{5,493},{6,494},{7,495},{8... | collective-permute-start | bytes 1032200 | tf_op jit(solution)/shard_map/ppermute | solution.py:172
  22.9 0.0 copy-start
  22.9 0.0 copy-start.1
  22.9 1.6 %collective-permute-start.2 = (bf16[448,384]{1,0:T(8,128)(2,1)}, bf16[448,384]{1,0:T(8,128)(2,1)S(1)}, u32[]{:S(2)}, u32[]{:S(2)}) collective-permute-start(bf16[448,384]{1,0:T(8,128)(2,1)} %get-tuple-element.14), channel_id=1, source_target_pairs={{0,480},{1,481},{2,482},{3,483},{4,484},{5,485},{6,486},{7,487},{8... | collective-permute-start | bytes 1032200 | tf_op jit(solution)/shard_map/ppermute | solution.py:172
  24.5 0.0 copy-done.2
  24.5 0.2 copy.36
  24.7 0.0 copy-done
  24.7 0.0 copy-done.1
  24.7 2.3 %forward_attention.3 = bf16[896,128]{1,0:T(8,128)(2,1)S(1)} custom-call(s32[1,2]{1,0:T(1,128)S(1)} %copy-done.1, s32[4,896]{1,0:T(4,128)S(1)} %copy-done, bf16[2,896,384]{2,1,0:T(8,128)(2,1)S(1)} %bitcast.40), custom_call_target="tpu_custom_call" | custom-call | flops 49999998976 | tf_op jit(solution)/shard_map/forward_attention/pallas_call | solution.py:113
  27.0 0.0 copy-start.3
  27.0 2.3 %forward_attention.2 = bf16[896,128]{1,0:T(8,128)(2,1)S(1)} custom-call(s32[1,2]{1,0:T(1,128)S(1)} %copy-done.1, s32[4,896]{1,0:T(4,128)S(1)} %copy-done, bf16[2,896,384]{2,1,0:T(8,128)(2,1)S(1)} %bitcast.41), custom_call_target="tpu_custom_call" | custom-call | flops 49999998976 | tf_op jit(solution)/shard_map/forward_attention/pallas_call | solution.py:113
  29.3 0.6 slice.10
  30.0 0.0 copy-done.3
  30.0 0.1 copy.37
  30.1 0.7 concatenate.4
  30.8 6.4 %collective-permute-start = (bf16[2,912,128]{2,1,0:T(8,128)(2,1)S(1)}, bf16[2,912,128]{2,1,0:T(8,128)(2,1)S(1)}, u32[]{:S(2)}, u32[]{:S(2)}) collective-permute-start(bf16[2,912,128]{2,1,0:T(8,128)(2,1)S(1)} %concatenate.4), channel_id=1, source_target_pairs={{16,0},{32,16},{48,32},{64,48},{80,64},{96,80},{112,96},{128,112},... | collective-permute-start | bytes 1400840 | tf_op jit(solution)/shard_map/ppermute | solution.py:162
  37.2 0.0 all-to-all-done.1
  37.2 0.9 slice_bitcast_fusion
  38.2 1.9 %collective-permute-start.5 = (bf16[4,2,56,384]{3,2,1,0:T(8,128)(2,1)}, bf16[4,2,56,384]{3,2,1,0:T(8,128)(2,1)S(1)}, u32[]{:S(2)}, u32[]{:S(2)}) collective-permute-start(bf16[4,2,56,384]{3,2,1,0:T(8,128)(2,1)} %get-tuple-element.16), channel_id=1, source_target_pairs={{0,492},{1,493},{2,494},{3,495},{4,480},{5,481},{6,482},{7,483},{8... | collective-permute-start | bytes 1032200 | tf_op jit(solution)/shard_map/ppermute | solution.py:172
  40.1 7.3 %collective-permute-start.4 = (bf16[4,2,56,384]{3,2,1,0:T(8,128)(2,1)}, bf16[4,2,56,384]{3,2,1,0:T(8,128)(2,1)S(1)}, u32[]{:S(2)}, u32[]{:S(2)}) collective-permute-start(bf16[4,2,56,384]{3,2,1,0:T(8,128)(2,1)} %get-tuple-element.17), channel_id=1, source_target_pairs={{0,484},{1,485},{2,486},{3,487},{4,488},{5,489},{6,490},{7,491},{8... | collective-permute-start | bytes 1032200 | tf_op jit(solution)/shard_map/ppermute | solution.py:172
  47.4 0.0 collective-permute-done.3.refs_1_
  47.4 0.0 collective-permute-done.2.refs_0_
  47.4 0.1 stacked.2
  47.4 0.7 copy.23
  48.2 1.0 copy.24
  49.2 4.2 %all-to-all-start = ((bf16[2,4,2,56,384]{4,3,2,0,1:T(8,128)(2,1)}), bf16[2,4,2,56,384]{4,3,2,0,1:T(8,128)(2,1)S(1)}, u32[]{:S(2)}, u32[]{:S(2)}) async-start(bf16[2,4,2,56,384]{4,3,2,0,1:T(8,128)(2,1)} %copy.24), calls=%async_computation | async-start | bytes 1376256 | tf_op jit(solution)/shard_map/all_to_all | solution.py:178
  53.4 35.8 %collective-permute-done.grad_ref = bf16[2,912,128]{2,1,0:T(8,128)(2,1)S(1)} collective-permute-done((bf16[2,912,128]{2,1,0:T(8,128)(2,1)S(1)}, bf16[2,912,128]{2,1,0:T(8,128)(2,1)S(1)}, u32[]{:S(2)}, u32[]{:S(2)}) %collective-permute-start) | collective-permute-done | bytes 466976 | tf_op jit(solution)/shard_map/ppermute | solution.py:162
  89.2 2.1 %collective-permute-start.1 = (bf16[2,896,128]{2,1,0:T(8,128)(2,1)S(1)}, bf16[2,896,128]{2,1,0:T(8,128)(2,1)S(1)}, u32[]{:S(2)}, u32[]{:S(2)}) collective-permute-start(bf16[2,896,128]{2,1,0:T(8,128)(2,1)S(1)} %pad_maximum_fusion), channel_id=1, source_target_pairs={{0,16},{16,32},{32,48},{48,64},{64,80},{80,96},{96,112},{112,128},... | collective-permute-start | bytes 1376264 | tf_op jit(solution)/shard_map/ppermute | solution.py:162
  91.3 0.0 collective-permute-done.5.refs_1_
  91.3 0.0 collective-permute-done.4.refs_0_
  91.3 0.1 stacked.3.late_ref
  91.3 0.0 all-to-all-done
  91.4 0.1 copy.29.early_ref
  91.4 7.1 %backward_attention.1 = bf16[2,896,384]{2,1,0:T(8,128)(2,1)S(1)} custom-call(s32[1]{0:T(128)} %bitcast.10.place_ref, s32[4,896]{1,0:T(4,128)S(1)} %copy-done, bf16[2,912,128]{2,1,0:T(8,128)(2,1)S(1)} %collective-permute-done.grad_ref, bf16[2,4,2,56,384]{4,3,2,1,0:T(8,128)(2,1)S(1)} %copy.29.early_ref, bf16[2,4,2,56,384]{4,3,2,1,0:T(8,128)(2,1)S(1)} %stacked.3.late_ref), custom_call_target="tpu_custom_call" | custom-call | tf_op jit(solution)/shard_map/backward_attention/pallas_call | solution.py:127
  98.5 2.5 %copy.31 = bf16[1,896,2,384]{3,2,1,0:T(2,128)(2,1)} copy(bf16[1,896,2,384]{3,1,2,0:T(8,128)(2,1)S(1)} %bitcast.39) | data formatting | bytes 2752512
  101.0 0.0 collective-permute-done.1
  101.0 1.2 %copy.30 = bf16[1,896,2,128]{3,2,1,0:T(2,128)(2,1)} copy(bf16[1,896,2,128]{3,1,2,0:T(8,128)(2,1)S(1)} %bitcast.48) | data formatting | bytes 917504
  (4 shorter events, 0.1 us)
Async XLA Ops:
  3.1 21.4 %copy-start.2 = (bf16[1,896,2,384]{3,2,1,0:T(2,128)(2,1)S(1)}, bf16[1,896,2,384]{3,2,1,0:T(2,128)(2,1)}, u32[]{:S(2)}) copy-start(bf16[1,896,2,384]{3,2,1,0:T(2,128)(2,1)} %param.5) | copy-start | bytes 4128772
  4.0 33.2 %all-to-all-start.1 = ((bf16[2,4,2,56,384]{4,3,2,0,1:T(8,128)(2,1)}), bf16[2,4,2,56,384]{4,3,2,0,1:T(8,128)(2,1)S(1)}, u32[]{:S(2)}, u32[]{:S(2)}) async-start(bf16[2,4,2,56,384]{4,3,2,0,1:T(8,128)(2,1)} %maximum_bitcast_fusion), calls=%async_computation.1 | async-start | bytes 1376256 | tf_op jit(solution)/shard_map/all_to_all | solution.py:178
  8.3 39.0 %collective-permute-start.3 = (bf16[448,384]{1,0:T(8,128)(2,1)}, bf16[448,384]{1,0:T(8,128)(2,1)S(1)}, u32[]{:S(2)}, u32[]{:S(2)}) collective-permute-start(bf16[448,384]{1,0:T(8,128)(2,1)} %get-tuple-element.13), channel_id=1, source_target_pairs={{0,488},{1,489},{2,490},{3,491},{4,492},{5,493},{6,494},{7,495},{8... | collective-permute-start | bytes 1032200 | tf_op jit(solution)/shard_map/ppermute | solution.py:172
  22.9 1.8 %copy-start = (s32[4,896]{1,0:T(4,128)S(1)}, s32[4,896]{1,0:T(4,128)}, u32[]{:S(2)}) copy-start(s32[4,896]{1,0:T(4,128)} %pos_ref.5) | copy-start | bytes 43012
  22.9 1.8 %copy-start.1 = (s32[1,2]{1,0:T(1,128)S(1)}, s32[1,2]{1,0:T(1,128)}, u32[]{:S(2)}) copy-start(s32[1,2]{1,0:T(1,128)} %which_ref.3) | copy-start | bytes 28
  22.9 24.5 %collective-permute-start.2 = (bf16[448,384]{1,0:T(8,128)(2,1)}, bf16[448,384]{1,0:T(8,128)(2,1)S(1)}, u32[]{:S(2)}, u32[]{:S(2)}) collective-permute-start(bf16[448,384]{1,0:T(8,128)(2,1)} %get-tuple-element.14), channel_id=1, source_target_pairs={{0,480},{1,481},{2,482},{3,483},{4,484},{5,485},{6,486},{7,487},{8... | collective-permute-start | bytes 1032200 | tf_op jit(solution)/shard_map/ppermute | solution.py:172
  27.0 3.0 %copy-start.3 = (bf16[1,896,2,128]{3,2,1,0:T(2,128)(2,1)S(1)}, bf16[1,896,2,128]{3,2,1,0:T(2,128)(2,1)}, u32[]{:S(2)}) copy-start(bf16[1,896,2,128]{3,2,1,0:T(2,128)(2,1)} %param.7) | copy-start | bytes 1376260
  30.8 58.3 %collective-permute-start = (bf16[2,912,128]{2,1,0:T(8,128)(2,1)S(1)}, bf16[2,912,128]{2,1,0:T(8,128)(2,1)S(1)}, u32[]{:S(2)}, u32[]{:S(2)}) collective-permute-start(bf16[2,912,128]{2,1,0:T(8,128)(2,1)S(1)} %concatenate.4), channel_id=1, source_target_pairs={{16,0},{32,16},{48,32},{64,48},{80,64},{96,80},{112,96},{128,112},... | collective-permute-start | bytes 1400840 | tf_op jit(solution)/shard_map/ppermute | solution.py:162
  38.2 53.1 %collective-permute-start.5 = (bf16[4,2,56,384]{3,2,1,0:T(8,128)(2,1)}, bf16[4,2,56,384]{3,2,1,0:T(8,128)(2,1)S(1)}, u32[]{:S(2)}, u32[]{:S(2)}) collective-permute-start(bf16[4,2,56,384]{3,2,1,0:T(8,128)(2,1)} %get-tuple-element.16), channel_id=1, source_target_pairs={{0,492},{1,493},{2,494},{3,495},{4,480},{5,481},{6,482},{7,483},{8... | collective-permute-start | bytes 1032200 | tf_op jit(solution)/shard_map/ppermute | solution.py:172
  40.1 51.2 %collective-permute-start.4 = (bf16[4,2,56,384]{3,2,1,0:T(8,128)(2,1)}, bf16[4,2,56,384]{3,2,1,0:T(8,128)(2,1)S(1)}, u32[]{:S(2)}, u32[]{:S(2)}) collective-permute-start(bf16[4,2,56,384]{3,2,1,0:T(8,128)(2,1)} %get-tuple-element.17), channel_id=1, source_target_pairs={{0,484},{1,485},{2,486},{3,487},{4,488},{5,489},{6,490},{7,491},{8... | collective-permute-start | bytes 1032200 | tf_op jit(solution)/shard_map/ppermute | solution.py:172
  49.2 42.2 %all-to-all-start = ((bf16[2,4,2,56,384]{4,3,2,0,1:T(8,128)(2,1)}), bf16[2,4,2,56,384]{4,3,2,0,1:T(8,128)(2,1)S(1)}, u32[]{:S(2)}, u32[]{:S(2)}) async-start(bf16[2,4,2,56,384]{4,3,2,0,1:T(8,128)(2,1)} %copy.24), calls=%async_computation | async-start | bytes 1376256 | tf_op jit(solution)/shard_map/all_to_all | solution.py:178
  89.2 11.9 %collective-permute-start.1 = (bf16[2,896,128]{2,1,0:T(8,128)(2,1)S(1)}, bf16[2,896,128]{2,1,0:T(8,128)(2,1)S(1)}, u32[]{:S(2)}, u32[]{:S(2)}) collective-permute-start(bf16[2,896,128]{2,1,0:T(8,128)(2,1)S(1)} %pad_maximum_fusion), channel_id=1, source_target_pairs={{0,16},{16,32},{32,48},{48,64},{64,80},{80,96},{96,112},{112,128},... | collective-permute-start | bytes 1376264 | tf_op jit(solution)/shard_map/ppermute | solution.py:162

commit v3 on v2

--- a/solution.py
+++ b/solution.py
@@ -10,6 +10,7 @@
 GROUPS = 4
 LANES = 4
 BLOCK = 128
+WIDE = 256
 FLOPS = 50_000_000_000
 FIRST = (0, 2, )
 LATE = (1, 3, )
@@ -59,48 +60,57 @@
 
 
 def backward_kernel(
-    place_ref, pos_ref, grad_ref, early_ref, late_ref, out_ref, rows_ref, dk_ref, dv_ref
+    place_ref, pos_ref, grad_ref, early_ref, late_ref, out_ref, rows_ref, probs_ref, scores_ref
 ):
     heads, count, width = out_ref.shape[0], out_ref.shape[1], grad_ref.shape[2]
     scale = width**-0.5
-    which = grad_ref[0, count : count + 1, :].astype(jnp.float32)
+    which = grad_ref[0, count : count + 1, :1].astype(jnp.float32)
     group = place_ref[0]
     piece = count // (GROUPS * LANES)
-    for head in range(heads):
-        for far in range(GROUPS):
-            for side in range(LANES):
-                source = lax.rem(group - far + GROUPS, GROUPS) * LANES + side
-                held, number = (early_ref, FIRST.index(far)) if far in FIRST else (late_ref, LATE.index(far))
-                rows_ref[pl.ds(pl.multiple_of(source * piece, 8), piece), :] = held[
-                    number, side, head
-                ].astype(jnp.float32)
-        keys_t = rows_ref[:, width : 2 * width].astype(jnp.bfloat16).T
-        for low in range(0, count, BLOCK):
-            high = low + BLOCK
-            query = rows_ref[low:high, :width].astype(jnp.bfloat16)
-            keys = rows_ref[:high, width : 2 * width].astype(jnp.bfloat16)
-            values = rows_ref[:high, 2 * width :].astype(jnp.bfloat16)
-            grad = grad_ref[head, low:high, :]
-            starts = document_starts(pos_ref, which, low, BLOCK)
+    for far in range(GROUPS):
+        held, number = (early_ref, FIRST.index(far)) if far in FIRST else (late_ref, LATE.index(far))
+        source = lax.rem(group - far + GROUPS, GROUPS) * LANES
+        for side in range(0, LANES, 2):
+            place = pl.ds(pl.multiple_of((source + side) * piece, 2 * piece), 2 * piece)
+            for head in range(heads):
+                both = [held[number, side + n, head].astype(jnp.float32) for n in range(2)]
+                rows_ref[head, place, :] = jnp.concatenate(both).astype(jnp.bfloat16)
+    keys_t = [rows_ref[head, :, width : 2 * width].T for head in range(heads)]
+    for low in range(0, count, WIDE):
+        high = min(low + WIDE, count)
+        starts = document_starts(pos_ref, which, low, high - low)
+        for head in range(heads):
+            query = rows_ref[head, low:high, :width]
+            keys = rows_ref[head, :high, width : 2 * width]
+            values = rows_ref[head, :high, 2 * width :]
             probs = probabilities(query, keys, starts, low, scale)
             grad_probs = lax.dot_general(
-                values, grad, (((1,), (1,)), ((), ())), preferred_element_type=jnp.float32
+                values,
+                grad_ref[head, low:high, :],
+                (((1,), (1,)), ((), ())),
+                preferred_element_type=jnp.float32,
             )
             delta = jnp.sum(probs * grad_probs, axis=0, keepdims=True)
             grad_scores = (probs * (grad_probs - delta) * scale).astype(jnp.bfloat16)
-            grad_values = jnp.dot(
-                probs.astype(jnp.bfloat16), grad, preferred_element_type=jnp.float32
+            probs_ref[head, :high, low:high] = probs.astype(jnp.bfloat16)
+            scores_ref[head, :high, low:high] = grad_scores
+            grad_query = jnp.dot(
+                keys_t[head][:, :high], grad_scores, preferred_element_type=jnp.float32
             )
-            grad_keys = jnp.dot(grad_scores, query, preferred_element_type=jnp.float32)
-            grad_query = jnp.dot(keys_t[:, :high], grad_scores, preferred_element_type=jnp.float32)
             out_ref[head, low:high, :width] = grad_query.T.astype(jnp.bfloat16)
-            if low > 0:
-                dv_ref[:low, :] += grad_values[:low]
-                dk_ref[:low, :] += grad_keys[:low]
-            dv_ref[low:high, :] = grad_values[low:]
-            dk_ref[low:high, :] = grad_keys[low:]
-        out_ref[head, :, width : 2 * width] = dk_ref[...].astype(jnp.bfloat16)
-        out_ref[head, :, 2 * width :] = dv_ref[...].astype(jnp.bfloat16)
+    for low in range(0, count, WIDE):
+        high = min(low + WIDE, count)
+        for head in range(heads):
+            out_ref[head, low:high, width : 2 * width] = jnp.dot(
+                scores_ref[head, low:high, low:],
+                rows_ref[head, low:, :width],
+                preferred_element_type=jnp.float32,
+            ).astype(jnp.bfloat16)
+            out_ref[head, low:high, 2 * width :] = jnp.dot(
+                probs_ref[head, low:high, low:],
+                grad_ref[head, low:count, :],
+                preferred_element_type=jnp.float32,
+            ).astype(jnp.bfloat16)
 
 
 SCALARS = pl.BlockSpec(memory_space=pltpu.SMEM)
@@ -130,9 +140,9 @@
         in_specs=[SCALARS] + [ARRAY] * 4,
         out_specs=ARRAY,
         scratch_shapes=[
-            pltpu.VMEM((count, 3 * width), jnp.float32),
-            pltpu.VMEM((count, width), jnp.float32),
-            pltpu.VMEM((count, width), jnp.float32),
+            pltpu.VMEM((heads, count, 3 * width), jnp.bfloat16),
+            pltpu.VMEM((heads, count, count), jnp.bfloat16),
+            pltpu.VMEM((heads, count, count), jnp.bfloat16),
         ],
         compiler_params=LIMIT,
         name="backward_attention",

time: 103 us -> 101 us (0.981)
  Pallas kernels: 11.8 us -> 10.2 us
    pallas_call x1, Pallas kernels: 7.1 us -> 5.51 us  [backward_of(): pl.pallas_call(backward_kernel, out_shape=jax.ShapeDtypeStruct((heads, co...]
  transfers between devices with their start and end apart: 8 -> 8, of which waited for: 1 -> 1; matrix products, arithmetic and copies ran while one was open for 7% -> 7% of each run, Pallas kernels for 12% -> 10%
where the time goes in v3:
time: 101 us
  starting transfers between devices  42.3 us (42%)
  waiting for transfers between devices  35.8 us (35%)
  local copies, waits for them, and re-layouts  10.4 us (10%)
  Pallas kernels  10.2 us (10%)
    ppermute x2, waiting for transfers between devices, passed_along(): return lax.ppermute(block, 'pipe', route)  35.8 us
    ppermute x4, starting transfers between devices, to_mirror(): return lax.ppermute(block, ('pipe', 'tensor'), route)  25.3 us
    all_to_all x2, starting transfers between devices, across_lanes(): lax.all_to_all(blocks, 'tensor', split_axis=1, concat_axis=1, axis_index_...  8.5 us
    ppermute x2, starting transfers between devices, passed_along(): return lax.ppermute(block, 'pipe', route)  8.47 us
    pallas_call x1, Pallas kernels, backward_of(): pl.pallas_call(backward_kernel, out_shape=jax.ShapeDtypeStruct((heads, co...  5.51 us
    pallas_call x2, Pallas kernels, forward_of(): pl.pallas_call(functools.partial(forward_kernel, head), out_shape=jax.Sha...  4.58 us
    unnamed x11, local copies, waits for them, and re-layouts  3.94 us
    dynamic_slice x3, local copies, waits for them, and re-layouts, for_group(): piece = lax.dynamic_slice_in_dim(held_stash[0], low, LANES * mine, 1)  2.37 us
  transfers between devices with their start and end apart: 8, of which 1 were waited for; matrix products, arithmetic and copies ran while one was open for 7% of the time, Pallas kernels for 10%

profile of v3, /device:TPU:59, one launch (start us, length us, event | category | flops | bytes accessed | tf_op | source)
XLA Modules:
  0.0 100.7 jit_solution(2947362074860097717)
XLA Ops:
  0.7 2.3 %constant_dynamic-slice_fusion.1 = (bf16[1,56,8,384]{3,2,1,0:T(8,128)(2,1)S(1)}, bf16[448,384]{1,0:T(8,128)(2,1)}, bf16[448,384]{1,0:T(8,128)(2,1)}, bf16[1,56,8,384]{3,2,1,0:T(8,128)(2,1)S(1)}) fusion(bf16[1,56,32,384]{3,2,1,0:T(8,128)(2,1)} %param.6, s32[]{:T(128)S(6)} %select_n.41, s32[]{:T(128)S(6)} %select_n.39, s32[]{:T(128)S(6)} %select_n.37, ...), kind=kLoop, calls=%fused_computation.9 | loop fusion | bytes 2752528 | tf_op jit(solution)/shard_map/dynamic_slice | solution.py:202
  3.1 0.0 copy-start.2
  3.1 0.9 maximum_bitcast_fusion
  4.0 4.3 %all-to-all-start.1 = ((bf16[2,4,2,56,384]{4,3,2,0,1:T(8,128)(2,1)}), bf16[2,4,2,56,384]{4,3,2,0,1:T(8,128)(2,1)S(1)}, u32[]{:S(2)}, u32[]{:S(2)}) async-start(bf16[2,4,2,56,384]{4,3,2,0,1:T(8,128)(2,1)} %maximum_bitcast_fusion), calls=%async_computation.1 | async-start | bytes 1376256 | tf_op jit(solution)/shard_map/all_to_all | solution.py:188
  8.3 14.5 %collective-permute-start.3 = (bf16[448,384]{1,0:T(8,128)(2,1)}, bf16[448,384]{1,0:T(8,128)(2,1)S(1)}, u32[]{:S(2)}, u32[]{:S(2)}) collective-permute-start(bf16[448,384]{1,0:T(8,128)(2,1)} %get-tuple-element.13), channel_id=1, source_target_pairs={{0,488},{1,489},{2,490},{3,491},{4,492},{5,493},{6,494},{7,495},{8... | collective-permute-start | bytes 1032200 | tf_op jit(solution)/shard_map/ppermute | solution.py:182
  22.9 0.0 copy-start
  22.9 0.0 copy-start.1
  22.9 1.6 %collective-permute-start.2 = (bf16[448,384]{1,0:T(8,128)(2,1)}, bf16[448,384]{1,0:T(8,128)(2,1)S(1)}, u32[]{:S(2)}, u32[]{:S(2)}) collective-permute-start(bf16[448,384]{1,0:T(8,128)(2,1)} %get-tuple-element.14), channel_id=1, source_target_pairs={{0,480},{1,481},{2,482},{3,483},{4,484},{5,485},{6,486},{7,487},{8... | collective-permute-start | bytes 1032200 | tf_op jit(solution)/shard_map/ppermute | solution.py:182
  24.5 0.0 copy-done.2
  24.5 0.2 copy.36
  24.7 0.0 copy-done
  24.7 0.0 copy-done.1
  24.7 2.3 %forward_attention.3 = bf16[896,128]{1,0:T(8,128)(2,1)S(1)} custom-call(s32[1,2]{1,0:T(1,128)S(1)} %copy-done.1, s32[4,896]{1,0:T(4,128)S(1)} %copy-done, bf16[2,896,384]{2,1,0:T(8,128)(2,1)S(1)} %bitcast.40), custom_call_target="tpu_custom_call" | custom-call | flops 49999998976 | tf_op jit(solution)/shard_map/forward_attention/pallas_call | solution.py:123
  27.0 0.0 copy-start.3
  27.0 2.3 %forward_attention.2 = bf16[896,128]{1,0:T(8,128)(2,1)S(1)} custom-call(s32[1,2]{1,0:T(1,128)S(1)} %copy-done.1, s32[4,896]{1,0:T(4,128)S(1)} %copy-done, bf16[2,896,384]{2,1,0:T(8,128)(2,1)S(1)} %bitcast.41), custom_call_target="tpu_custom_call" | custom-call | flops 49999998976 | tf_op jit(solution)/shard_map/forward_attention/pallas_call | solution.py:123
  29.3 0.6 slice.10
  30.0 0.0 copy-done.3
  30.0 0.1 copy.37
  30.1 0.7 concatenate.4
  30.8 6.4 %collective-permute-start = (bf16[2,912,128]{2,1,0:T(8,128)(2,1)S(1)}, bf16[2,912,128]{2,1,0:T(8,128)(2,1)S(1)}, u32[]{:S(2)}, u32[]{:S(2)}) collective-permute-start(bf16[2,912,128]{2,1,0:T(8,128)(2,1)S(1)} %concatenate.4), channel_id=1, source_target_pairs={{16,0},{32,16},{48,32},{64,48},{80,64},{96,80},{112,96},{128,112},... | collective-permute-start | bytes 1400840 | tf_op jit(solution)/shard_map/ppermute | solution.py:172
  37.2 0.0 all-to-all-done.1
  37.2 0.9 slice_bitcast_fusion
  38.2 1.9 %collective-permute-start.5 = (bf16[4,2,56,384]{3,2,1,0:T(8,128)(2,1)}, bf16[4,2,56,384]{3,2,1,0:T(8,128)(2,1)S(1)}, u32[]{:S(2)}, u32[]{:S(2)}) collective-permute-start(bf16[4,2,56,384]{3,2,1,0:T(8,128)(2,1)} %get-tuple-element.16), channel_id=1, source_target_pairs={{0,492},{1,493},{2,494},{3,495},{4,480},{5,481},{6,482},{7,483},{8... | collective-permute-start | bytes 1032200 | tf_op jit(solution)/shard_map/ppermute | solution.py:182
  40.1 7.3 %collective-permute-start.4 = (bf16[4,2,56,384]{3,2,1,0:T(8,128)(2,1)}, bf16[4,2,56,384]{3,2,1,0:T(8,128)(2,1)S(1)}, u32[]{:S(2)}, u32[]{:S(2)}) collective-permute-start(bf16[4,2,56,384]{3,2,1,0:T(8,128)(2,1)} %get-tuple-element.17), channel_id=1, source_target_pairs={{0,484},{1,485},{2,486},{3,487},{4,488},{5,489},{6,490},{7,491},{8... | collective-permute-start | bytes 1032200 | tf_op jit(solution)/shard_map/ppermute | solution.py:182
  47.4 0.0 collective-permute-done.3.refs_1_
  47.4 0.0 collective-permute-done.2.refs_0_
  47.4 0.1 stacked.2
  47.4 0.7 copy.23
  48.2 1.0 copy.24
  49.2 4.2 %all-to-all-start = ((bf16[2,4,2,56,384]{4,3,2,0,1:T(8,128)(2,1)}), bf16[2,4,2,56,384]{4,3,2,0,1:T(8,128)(2,1)S(1)}, u32[]{:S(2)}, u32[]{:S(2)}) async-start(bf16[2,4,2,56,384]{4,3,2,0,1:T(8,128)(2,1)} %copy.24), calls=%async_computation | async-start | bytes 1376256 | tf_op jit(solution)/shard_map/all_to_all | solution.py:188
  53.4 35.8 %collective-permute-done.grad_ref = bf16[2,912,128]{2,1,0:T(8,128)(2,1)S(1)} collective-permute-done((bf16[2,912,128]{2,1,0:T(8,128)(2,1)S(1)}, bf16[2,912,128]{2,1,0:T(8,128)(2,1)S(1)}, u32[]{:S(2)}, u32[]{:S(2)}) %collective-permute-start) | collective-permute-done | bytes 466976 | tf_op jit(solution)/shard_map/ppermute | solution.py:172
  89.2 2.1 %collective-permute-start.1 = (bf16[2,896,128]{2,1,0:T(8,128)(2,1)S(1)}, bf16[2,896,128]{2,1,0:T(8,128)(2,1)S(1)}, u32[]{:S(2)}, u32[]{:S(2)}) collective-permute-start(bf16[2,896,128]{2,1,0:T(8,128)(2,1)S(1)} %pad_maximum_fusion), channel_id=1, source_target_pairs={{0,16},{16,32},{32,48},{48,64},{64,80},{80,96},{96,112},{112,128},... | collective-permute-start | bytes 1376264 | tf_op jit(solution)/shard_map/ppermute | solution.py:172
  91.3 0.0 collective-permute-done.5.refs_1_
  91.3 0.0 collective-permute-done.4.refs_0_
  91.3 0.1 stacked.3.late_ref
  91.3 0.0 all-to-all-done
  91.4 0.1 copy.29.early_ref
  91.4 5.5 %backward_attention.1 = bf16[2,896,384]{2,1,0:T(8,128)(2,1)S(1)} custom-call(s32[1]{0:T(128)} %bitcast.10.place_ref, s32[4,896]{1,0:T(4,128)S(1)} %copy-done, bf16[2,912,128]{2,1,0:T(8,128)(2,1)S(1)} %collective-permute-done.grad_ref, bf16[2,4,2,56,384]{4,3,2,1,0:T(8,128)(2,1)S(1)} %copy.29.early_ref, bf16[2,4,2,56,384]{4,3,2,1,0:T(8,128)(2,1)S(1)} %stacked.3.late_ref), custom_call_target="tpu_custom_call" | custom-call | tf_op jit(solution)/shard_map/backward_attention/pallas_call | solution.py:137
  97.0 2.5 %copy.31 = bf16[1,896,2,384]{3,2,1,0:T(2,128)(2,1)} copy(bf16[1,896,2,384]{3,1,2,0:T(8,128)(2,1)S(1)} %bitcast.39) | data formatting | bytes 2752512
  99.5 0.0 collective-permute-done.1
  99.5 1.2 %copy.30 = bf16[1,896,2,128]{3,2,1,0:T(2,128)(2,1)} copy(bf16[1,896,2,128]{3,1,2,0:T(8,128)(2,1)S(1)} %bitcast.48) | data formatting | bytes 917504
  (4 shorter events, 0.1 us)
Async XLA Ops:
  3.1 21.4 %copy-start.2 = (bf16[1,896,2,384]{3,2,1,0:T(2,128)(2,1)S(1)}, bf16[1,896,2,384]{3,2,1,0:T(2,128)(2,1)}, u32[]{:S(2)}) copy-start(bf16[1,896,2,384]{3,2,1,0:T(2,128)(2,1)} %param.5) | copy-start | bytes 4128772
  4.0 33.2 %all-to-all-start.1 = ((bf16[2,4,2,56,384]{4,3,2,0,1:T(8,128)(2,1)}), bf16[2,4,2,56,384]{4,3,2,0,1:T(8,128)(2,1)S(1)}, u32[]{:S(2)}, u32[]{:S(2)}) async-start(bf16[2,4,2,56,384]{4,3,2,0,1:T(8,128)(2,1)} %maximum_bitcast_fusion), calls=%async_computation.1 | async-start | bytes 1376256 | tf_op jit(solution)/shard_map/all_to_all | solution.py:188
  8.3 39.0 %collective-permute-start.3 = (bf16[448,384]{1,0:T(8,128)(2,1)}, bf16[448,384]{1,0:T(8,128)(2,1)S(1)}, u32[]{:S(2)}, u32[]{:S(2)}) collective-permute-start(bf16[448,384]{1,0:T(8,128)(2,1)} %get-tuple-element.13), channel_id=1, source_target_pairs={{0,488},{1,489},{2,490},{3,491},{4,492},{5,493},{6,494},{7,495},{8... | collective-permute-start | bytes 1032200 | tf_op jit(solution)/shard_map/ppermute | solution.py:182
  22.9 1.8 %copy-start = (s32[4,896]{1,0:T(4,128)S(1)}, s32[4,896]{1,0:T(4,128)}, u32[]{:S(2)}) copy-start(s32[4,896]{1,0:T(4,128)} %pos_ref.5) | copy-start | bytes 43012
  22.9 1.8 %copy-start.1 = (s32[1,2]{1,0:T(1,128)S(1)}, s32[1,2]{1,0:T(1,128)}, u32[]{:S(2)}) copy-start(s32[1,2]{1,0:T(1,128)} %which_ref.3) | copy-start | bytes 28
  22.9 24.5 %collective-permute-start.2 = (bf16[448,384]{1,0:T(8,128)(2,1)}, bf16[448,384]{1,0:T(8,128)(2,1)S(1)}, u32[]{:S(2)}, u32[]{:S(2)}) collective-permute-start(bf16[448,384]{1,0:T(8,128)(2,1)} %get-tuple-element.14), channel_id=1, source_target_pairs={{0,480},{1,481},{2,482},{3,483},{4,484},{5,485},{6,486},{7,487},{8... | collective-permute-start | bytes 1032200 | tf_op jit(solution)/shard_map/ppermute | solution.py:182
  27.0 3.0 %copy-start.3 = (bf16[1,896,2,128]{3,2,1,0:T(2,128)(2,1)S(1)}, bf16[1,896,2,128]{3,2,1,0:T(2,128)(2,1)}, u32[]{:S(2)}) copy-start(bf16[1,896,2,128]{3,2,1,0:T(2,128)(2,1)} %param.7) | copy-start | bytes 1376260
  30.8 58.3 %collective-permute-start = (bf16[2,912,128]{2,1,0:T(8,128)(2,1)S(1)}, bf16[2,912,128]{2,1,0:T(8,128)(2,1)S(1)}, u32[]{:S(2)}, u32[]{:S(2)}) collective-permute-start(bf16[2,912,128]{2,1,0:T(8,128)(2,1)S(1)} %concatenate.4), channel_id=1, source_target_pairs={{16,0},{32,16},{48,32},{64,48},{80,64},{96,80},{112,96},{128,112},... | collective-permute-start | bytes 1400840 | tf_op jit(solution)/shard_map/ppermute | solution.py:172
  38.2 53.1 %collective-permute-start.5 = (bf16[4,2,56,384]{3,2,1,0:T(8,128)(2,1)}, bf16[4,2,56,384]{3,2,1,0:T(8,128)(2,1)S(1)}, u32[]{:S(2)}, u32[]{:S(2)}) collective-permute-start(bf16[4,2,56,384]{3,2,1,0:T(8,128)(2,1)} %get-tuple-element.16), channel_id=1, source_target_pairs={{0,492},{1,493},{2,494},{3,495},{4,480},{5,481},{6,482},{7,483},{8... | collective-permute-start | bytes 1032200 | tf_op jit(solution)/shard_map/ppermute | solution.py:182
  40.1 51.2 %collective-permute-start.4 = (bf16[4,2,56,384]{3,2,1,0:T(8,128)(2,1)}, bf16[4,2,56,384]{3,2,1,0:T(8,128)(2,1)S(1)}, u32[]{:S(2)}, u32[]{:S(2)}) collective-permute-start(bf16[4,2,56,384]{3,2,1,0:T(8,128)(2,1)} %get-tuple-element.17), channel_id=1, source_target_pairs={{0,484},{1,485},{2,486},{3,487},{4,488},{5,489},{6,490},{7,491},{8... | collective-permute-start | bytes 1032200 | tf_op jit(solution)/shard_map/ppermute | solution.py:182
  49.2 42.2 %all-to-all-start = ((bf16[2,4,2,56,384]{4,3,2,0,1:T(8,128)(2,1)}), bf16[2,4,2,56,384]{4,3,2,0,1:T(8,128)(2,1)S(1)}, u32[]{:S(2)}, u32[]{:S(2)}) async-start(bf16[2,4,2,56,384]{4,3,2,0,1:T(8,128)(2,1)} %copy.24), calls=%async_computation | async-start | bytes 1376256 | tf_op jit(solution)/shard_map/all_to_all | solution.py:188
  89.2 10.3 %collective-permute-start.1 = (bf16[2,896,128]{2,1,0:T(8,128)(2,1)S(1)}, bf16[2,896,128]{2,1,0:T(8,128)(2,1)S(1)}, u32[]{:S(2)}, u32[]{:S(2)}) collective-permute-start(bf16[2,896,128]{2,1,0:T(8,128)(2,1)S(1)} %pad_maximum_fusion), channel_id=1, source_target_pairs={{0,16},{16,32},{32,48},{48,64},{64,80},{80,96},{96,112},{112,128},... | collective-permute-start | bytes 1376264 | tf_op jit(solution)/shard_map/ppermute | solution.py:172

commit v4 on v3

--- a/solution.py
+++ b/solution.py
@@ -12,7 +12,7 @@
 BLOCK = 128
 WIDE = 256
 FLOPS = 50_000_000_000
-FIRST = (0, 2, )
+FIRST = (2, 0)
 LATE = (1, 3, )
 
 
@@ -217,9 +217,10 @@
     attn_out = jnp.stack([forward_of(head, plan, positions, packed) for head in range(mine)])
     which = jnp.broadcast_to(plan[0, 1].astype(jnp.bfloat16), (mine, 16, d_out.shape[3]))
     grad_out = passed_along(jnp.concatenate([after(d_out, attn_out)[0].transpose(1, 0, 2), which], axis=1), -1)
-    to_next = passed_along(after(attn_out, grad_out), 1).transpose(1, 0, 2)
+    to_next = passed_along(after(attn_out, first), 1)
     place = group.astype(jnp.int32)[None]
     grads = backward_of(place, positions, grad_out, early, late)
+    to_next = after(to_next, grads).transpose(1, 0, 2)
     return to_next[None], grads.transpose(1, 0, 2)[None]
 
 

time: 101 us -> 103 us (1.020)
  the two profiles are of different devices: /device:TPU:59 before, /device:TPU:64 now
where the time goes in v4:
time: 103 us; the launch traced here: 102 us
  starting transfers between devices  64.5 us (63%)
  waiting for transfers between devices  13.9 us (13%)
  local copies, waits for them, and re-layouts  11.9 us (12%)
  Pallas kernels  10.2 us (10%)
    ppermute x4, starting transfers between devices, to_mirror(): return lax.ppermute(block, ('pipe', 'tensor'), route)  31.2 us
    ppermute x2, starting transfers between devices, passed_along(): return lax.ppermute(block, 'pipe', route)  22.6 us
    all_to_all x2, starting transfers between devices, across_lanes(): lax.all_to_all(blocks, 'tensor', split_axis=1, concat_axis=1, axis_index_...  10.6 us
    all_to_all x2, waiting for transfers between devices, across_lanes(): lax.all_to_all(blocks, 'tensor', split_axis=1, concat_axis=1, axis_index_...  8.63 us
    pallas_call x1, Pallas kernels, backward_of(): pl.pallas_call(backward_kernel, out_shape=jax.ShapeDtypeStruct((heads, co...  5.52 us
    unnamed x11, local copies, waits for them, and re-layouts  5.47 us
    ppermute x4, waiting for transfers between devices, to_mirror(): return lax.ppermute(block, ('pipe', 'tensor'), route)  5.24 us
    pallas_call x2, Pallas kernels, forward_of(): pl.pallas_call(functools.partial(forward_kernel, head), out_shape=jax.Sha...  4.58 us
  transfers between devices with their start and end apart: 8, of which 4 were waited for; matrix products, arithmetic and copies ran while one was open for 5% of the time, Pallas kernels for 10%

profile of v4, /device:TPU:64, one launch (start us, length us, event | category | flops | bytes accessed | tf_op | source)
XLA Modules:
  0.0 102.4 jit_solution(13884581897537494155)
XLA Ops:
  0.7 2.3 %constant_dynamic-slice_fusion.1 = (bf16[1,56,8,384]{3,2,1,0:T(8,128)(2,1)S(1)}, bf16[448,384]{1,0:T(8,128)(2,1)}, bf16[448,384]{1,0:T(8,128)(2,1)}, bf16[1,56,8,384]{3,2,1,0:T(8,128)(2,1)S(1)}) fusion(bf16[1,56,32,384]{3,2,1,0:T(8,128)(2,1)} %param.6, s32[]{:T(128)S(6)} %select_n.41, s32[]{:T(128)S(6)} %select_n.39, s32[]{:T(128)S(6)} %select_n.37, ...), kind=kLoop, calls=%fused_computation.9 | loop fusion | bytes 2752528 | tf_op jit(solution)/shard_map/dynamic_slice | solution.py:202
  3.0 15.9 %collective-permute-start = (bf16[448,384]{1,0:T(8,128)(2,1)}, bf16[448,384]{1,0:T(8,128)(2,1)S(1)}, u32[]{:S(2)}, u32[]{:S(2)}) collective-permute-start(bf16[448,384]{1,0:T(8,128)(2,1)} %get-tuple-element.16), channel_id=1, source_target_pairs={{0,488},{1,489},{2,490},{3,491},{4,492},{5,493},{6,494},{7,495},{8... | collective-permute-start | bytes 1032200 | tf_op jit(solution)/shard_map/ppermute | solution.py:182
  18.9 2.6 %collective-permute-start.1 = (bf16[448,384]{1,0:T(8,128)(2,1)}, bf16[448,384]{1,0:T(8,128)(2,1)S(1)}, u32[]{:S(2)}, u32[]{:S(2)}) collective-permute-start(bf16[448,384]{1,0:T(8,128)(2,1)} %get-tuple-element.15), channel_id=1, source_target_pairs={{0,480},{1,481},{2,482},{3,483},{4,484},{5,485},{6,486},{7,487},{8... | collective-permute-start | bytes 1032200 | tf_op jit(solution)/shard_map/ppermute | solution.py:182
  21.6 0.0 copy-start.2
  21.6 0.9 maximum_bitcast_fusion
  22.6 4.3 %all-to-all-start.1 = ((bf16[2,4,2,56,384]{4,3,2,0,1:T(8,128)(2,1)}), bf16[2,4,2,56,384]{4,3,2,0,1:T(8,128)(2,1)S(1)}, u32[]{:S(2)}, u32[]{:S(2)}) async-start(bf16[2,4,2,56,384]{4,3,2,0,1:T(8,128)(2,1)} %maximum_bitcast_fusion), calls=%async_computation.1 | async-start | bytes 1376256 | tf_op jit(solution)/shard_map/all_to_all | solution.py:188
  26.9 0.0 copy-done.2
  26.9 0.0 copy-start
  26.9 0.0 copy-start.1
  26.9 0.2 copy.36
  27.1 0.5 copy-done
  27.6 0.0 copy-done.1
  27.6 2.3 %forward_attention.3 = bf16[896,128]{1,0:T(8,128)(2,1)S(1)} custom-call(s32[1,2]{1,0:T(1,128)S(1)} %copy-done.1, s32[4,896]{1,0:T(4,128)S(1)} %copy-done, bf16[2,896,384]{2,1,0:T(8,128)(2,1)S(1)} %bitcast.40), custom_call_target="tpu_custom_call" | custom-call | flops 49999998976 | tf_op jit(solution)/shard_map/forward_attention/pallas_call | solution.py:123
  29.9 0.0 copy-start.3
  29.9 2.3 %forward_attention.2 = bf16[896,128]{1,0:T(8,128)(2,1)S(1)} custom-call(s32[1,2]{1,0:T(1,128)S(1)} %copy-done.1, s32[4,896]{1,0:T(4,128)S(1)} %copy-done, bf16[2,896,384]{2,1,0:T(8,128)(2,1)S(1)} %bitcast.41), custom_call_target="tpu_custom_call" | custom-call | flops 49999998976 | tf_op jit(solution)/shard_map/forward_attention/pallas_call | solution.py:123
  32.2 0.0 copy-done.3
  32.3 0.1 copy.37
  32.3 0.6 slice.10
  33.0 0.7 concatenate.4
  33.7 1.9 %collective-permute-start.3 = (bf16[2,912,128]{2,1,0:T(8,128)(2,1)S(1)}, bf16[2,912,128]{2,1,0:T(8,128)(2,1)S(1)}, u32[]{:S(2)}, u32[]{:S(2)}) collective-permute-start(bf16[2,912,128]{2,1,0:T(8,128)(2,1)S(1)} %concatenate.4), channel_id=1, source_target_pairs={{16,0},{32,16},{48,32},{64,48},{80,64},{96,80},{112,96},{128,112},... | collective-permute-start | bytes 1400840 | tf_op jit(solution)/shard_map/ppermute | solution.py:172
  35.6 2.2 %all-to-all-done.1 = bf16[2,4,2,56,384]{4,3,2,0,1:T(8,128)(2,1)S(1)} async-done(((bf16[2,4,2,56,384]{4,3,2,0,1:T(8,128)(2,1)}), bf16[2,4,2,56,384]{4,3,2,0,1:T(8,128)(2,1)S(1)}, u32[]{:S(2)}, u32[]{:S(2)}) %all-to-all-start.1) | async-done | bytes 688160 | tf_op jit(solution)/shard_map/all_to_all | solution.py:188
  37.8 0.9 slice_bitcast_fusion
  38.7 4.3 %collective-permute-start.4 = (bf16[4,2,56,384]{3,2,1,0:T(8,128)(2,1)}, bf16[4,2,56,384]{3,2,1,0:T(8,128)(2,1)S(1)}, u32[]{:S(2)}, u32[]{:S(2)}) collective-permute-start(bf16[4,2,56,384]{3,2,1,0:T(8,128)(2,1)} %get-tuple-element.19), channel_id=1, source_target_pairs={{0,484},{1,485},{2,486},{3,487},{4,488},{5,489},{6,490},{7,491},{8... | collective-permute-start | bytes 1032200 | tf_op jit(solution)/shard_map/ppermute | solution.py:182
  43.0 8.5 %collective-permute-start.5 = (bf16[4,2,56,384]{3,2,1,0:T(8,128)(2,1)}, bf16[4,2,56,384]{3,2,1,0:T(8,128)(2,1)S(1)}, u32[]{:S(2)}, u32[]{:S(2)}) collective-permute-start(bf16[4,2,56,384]{3,2,1,0:T(8,128)(2,1)} %get-tuple-element.18), channel_id=1, source_target_pairs={{0,492},{1,493},{2,494},{3,495},{4,480},{5,481},{6,482},{7,483},{8... | collective-permute-start | bytes 1032200 | tf_op jit(solution)/shard_map/ppermute | solution.py:182
  51.5 0.0 collective-permute-done.refs_0_
  51.5 0.3 collective-permute-done.1.refs_1_
  51.8 0.1 stacked.2
  51.9 0.7 copy.23
  52.6 20.7 %collective-permute-start.2 = (bf16[2,896,128]{2,1,0:T(8,128)(2,1)S(1)}, bf16[2,896,128]{2,1,0:T(8,128)(2,1)}, u32[]{:S(2)}, u32[]{:S(2)}) collective-permute-start(bf16[2,896,128]{2,1,0:T(8,128)(2,1)S(1)} %pad_maximum_fusion), channel_id=1, source_target_pairs={{0,16},{16,32},{32,48},{48,64},{64,80},{80,96},{96,112},{112,128},... | collective-permute-start | bytes 1376264 | tf_op jit(solution)/shard_map/ppermute | solution.py:172
  73.3 1.0 copy.24
  74.3 6.3 %all-to-all-start = ((bf16[2,4,2,56,384]{4,3,2,0,1:T(8,128)(2,1)}), bf16[2,4,2,56,384]{4,3,2,0,1:T(8,128)(2,1)S(1)}, u32[]{:S(2)}, u32[]{:S(2)}) async-start(bf16[2,4,2,56,384]{4,3,2,0,1:T(8,128)(2,1)} %copy.24), calls=%async_computation | async-start | bytes 1376256 | tf_op jit(solution)/shard_map/all_to_all | solution.py:188
  80.6 0.0 collective-permute-done.4.refs_0_
  80.6 4.9 %collective-permute-done.5.refs_1_ = bf16[4,2,56,384]{3,2,1,0:T(8,128)(2,1)S(1)} collective-permute-done((bf16[4,2,56,384]{3,2,1,0:T(8,128)(2,1)}, bf16[4,2,56,384]{3,2,1,0:T(8,128)(2,1)S(1)}, u32[]{:S(2)}, u32[]{:S(2)}) %collective-permute-start.5) | collective-permute-done | bytes 344096 | tf_op jit(solution)/shard_map/ppermute | solution.py:182
  85.6 0.1 stacked.3.late_ref
  85.6 6.4 %all-to-all-done = bf16[2,4,2,56,384]{4,3,2,0,1:T(8,128)(2,1)S(1)} async-done(((bf16[2,4,2,56,384]{4,3,2,0,1:T(8,128)(2,1)}), bf16[2,4,2,56,384]{4,3,2,0,1:T(8,128)(2,1)S(1)}, u32[]{:S(2)}, u32[]{:S(2)}) %all-to-all-start) | async-done | bytes 688160 | tf_op jit(solution)/shard_map/all_to_all | solution.py:188
  92.1 0.1 copy.29.early_ref
  92.1 0.0 collective-permute-done.3.grad_ref
  92.1 5.5 %backward_attention.1 = bf16[2,896,384]{2,1,0:T(8,128)(2,1)S(1)} custom-call(s32[1]{0:T(128)} %bitcast.7.place_ref, s32[4,896]{1,0:T(4,128)S(1)} %copy-done, bf16[2,912,128]{2,1,0:T(8,128)(2,1)S(1)} %collective-permute-done.3.grad_ref, bf16[2,4,2,56,384]{4,3,2,1,0:T(8,128)(2,1)S(1)} %copy.29.early_ref, bf16[2,4,2,56,384]{4,3,2,1,0:T(8,128)(2,1)S(1)} %stacked.3.late_ref), custom_call_target="tpu_custom_call" | custom-call | tf_op jit(solution)/shard_map/backward_attention/pallas_call | solution.py:137
  97.7 0.0 collective-permute-done.2
  97.7 2.3 %copy.30 = bf16[1,896,2,128]{3,2,1,0:T(2,128)(2,1)} copy(bf16[1,896,2,128]{3,1,2,0:T(8,128)(2,1)} %bitcast.19) | data formatting | bytes 917504
  99.9 2.5 %copy.31 = bf16[1,896,2,384]{3,2,1,0:T(2,128)(2,1)} copy(bf16[1,896,2,384]{3,1,2,0:T(8,128)(2,1)S(1)} %bitcast.39) | data formatting | bytes 2752512
  (4 shorter events, 0.1 us)
Async XLA Ops:
  3.0 48.5 %collective-permute-start = (bf16[448,384]{1,0:T(8,128)(2,1)}, bf16[448,384]{1,0:T(8,128)(2,1)S(1)}, u32[]{:S(2)}, u32[]{:S(2)}) collective-permute-start(bf16[448,384]{1,0:T(8,128)(2,1)} %get-tuple-element.16), channel_id=1, source_target_pairs={{0,488},{1,489},{2,490},{3,491},{4,492},{5,493},{6,494},{7,495},{8... | collective-permute-start | bytes 1032200 | tf_op jit(solution)/shard_map/ppermute | solution.py:182
  18.9 32.9 %collective-permute-start.1 = (bf16[448,384]{1,0:T(8,128)(2,1)}, bf16[448,384]{1,0:T(8,128)(2,1)S(1)}, u32[]{:S(2)}, u32[]{:S(2)}) collective-permute-start(bf16[448,384]{1,0:T(8,128)(2,1)} %get-tuple-element.15), channel_id=1, source_target_pairs={{0,480},{1,481},{2,482},{3,483},{4,484},{5,485},{6,486},{7,487},{8... | collective-permute-start | bytes 1032200 | tf_op jit(solution)/shard_map/ppermute | solution.py:182
  21.6 5.2 %copy-start.2 = (bf16[1,896,2,384]{3,2,1,0:T(2,128)(2,1)S(1)}, bf16[1,896,2,384]{3,2,1,0:T(2,128)(2,1)}, u32[]{:S(2)}) copy-start(bf16[1,896,2,384]{3,2,1,0:T(2,128)(2,1)} %param.5) | copy-start | bytes 4128772
  22.6 15.3 %all-to-all-start.1 = ((bf16[2,4,2,56,384]{4,3,2,0,1:T(8,128)(2,1)}), bf16[2,4,2,56,384]{4,3,2,0,1:T(8,128)(2,1)S(1)}, u32[]{:S(2)}, u32[]{:S(2)}) async-start(bf16[2,4,2,56,384]{4,3,2,0,1:T(8,128)(2,1)} %maximum_bitcast_fusion), calls=%async_computation.1 | async-start | bytes 1376256 | tf_op jit(solution)/shard_map/all_to_all | solution.py:188
  26.9 0.7 copy-start
  26.9 0.7 copy-start.1
  29.9 2.4 %copy-start.3 = (bf16[1,896,2,128]{3,2,1,0:T(2,128)(2,1)S(1)}, bf16[1,896,2,128]{3,2,1,0:T(2,128)(2,1)}, u32[]{:S(2)}) copy-start(bf16[1,896,2,128]{3,2,1,0:T(2,128)(2,1)} %param.7) | copy-start | bytes 1376260
  33.7 58.5 %collective-permute-start.3 = (bf16[2,912,128]{2,1,0:T(8,128)(2,1)S(1)}, bf16[2,912,128]{2,1,0:T(8,128)(2,1)S(1)}, u32[]{:S(2)}, u32[]{:S(2)}) collective-permute-start(bf16[2,912,128]{2,1,0:T(8,128)(2,1)S(1)} %concatenate.4), channel_id=1, source_target_pairs={{16,0},{32,16},{48,32},{64,48},{80,64},{96,80},{112,96},{128,112},... | collective-permute-start | bytes 1400840 | tf_op jit(solution)/shard_map/ppermute | solution.py:172
  38.7 41.9 %collective-permute-start.4 = (bf16[4,2,56,384]{3,2,1,0:T(8,128)(2,1)}, bf16[4,2,56,384]{3,2,1,0:T(8,128)(2,1)S(1)}, u32[]{:S(2)}, u32[]{:S(2)}) collective-permute-start(bf16[4,2,56,384]{3,2,1,0:T(8,128)(2,1)} %get-tuple-element.19), channel_id=1, source_target_pairs={{0,484},{1,485},{2,486},{3,487},{4,488},{5,489},{6,490},{7,491},{8... | collective-permute-start | bytes 1032200 | tf_op jit(solution)/shard_map/ppermute | solution.py:182
  43.0 42.6 %collective-permute-start.5 = (bf16[4,2,56,384]{3,2,1,0:T(8,128)(2,1)}, bf16[4,2,56,384]{3,2,1,0:T(8,128)(2,1)S(1)}, u32[]{:S(2)}, u32[]{:S(2)}) collective-permute-start(bf16[4,2,56,384]{3,2,1,0:T(8,128)(2,1)} %get-tuple-element.18), channel_id=1, source_target_pairs={{0,492},{1,493},{2,494},{3,495},{4,480},{5,481},{6,482},{7,483},{8... | collective-permute-start | bytes 1032200 | tf_op jit(solution)/shard_map/ppermute | solution.py:182
  52.6 45.1 %collective-permute-start.2 = (bf16[2,896,128]{2,1,0:T(8,128)(2,1)S(1)}, bf16[2,896,128]{2,1,0:T(8,128)(2,1)}, u32[]{:S(2)}, u32[]{:S(2)}) collective-permute-start(bf16[2,896,128]{2,1,0:T(8,128)(2,1)S(1)} %pad_maximum_fusion), channel_id=1, source_target_pairs={{0,16},{16,32},{32,48},{48,64},{64,80},{80,96},{96,112},{112,128},... | collective-permute-start | bytes 1376264 | tf_op jit(solution)/shard_map/ppermute | solution.py:172
  74.3 17.7 %all-to-all-start = ((bf16[2,4,2,56,384]{4,3,2,0,1:T(8,128)(2,1)}), bf16[2,4,2,56,384]{4,3,2,0,1:T(8,128)(2,1)S(1)}, u32[]{:S(2)}, u32[]{:S(2)}) async-start(bf16[2,4,2,56,384]{4,3,2,0,1:T(8,128)(2,1)} %copy.24), calls=%async_computation | async-start | bytes 1376256 | tf_op jit(solution)/shard_map/all_to_all | solution.py:188

commit v5 on v3

--- a/solution.py
+++ b/solution.py
@@ -13,7 +13,7 @@
 WIDE = 256
 FLOPS = 50_000_000_000
 FIRST = (0, 2, )
-LATE = (1, 3, )
+LATE = (3, 1)
 
 
 def visible_in(start, low, width, count):

time: 101 us -> 105 us (1.040)
  the two profiles are of different devices: /device:TPU:59 before, /device:TPU:48 now
where the time goes in v5:
time: 105 us; the launch traced here: 104 us
  waiting for transfers between devices  41 us (39%)
  starting transfers between devices  40.8 us (39%)
  local copies, waits for them, and re-layouts  10.4 us (10%)
  Pallas kernels  10.2 us (10%)
    ppermute x4, waiting for transfers between devices, to_mirror(): return lax.ppermute(block, ('pipe', 'tensor'), route)  34.2 us
    ppermute x4, starting transfers between devices, to_mirror(): return lax.ppermute(block, ('pipe', 'tensor'), route)  27.9 us
    all_to_all x2, starting transfers between devices, across_lanes(): lax.all_to_all(blocks, 'tensor', split_axis=1, concat_axis=1, axis_index_...  8.84 us
    all_to_all x2, waiting for transfers between devices, across_lanes(): lax.all_to_all(blocks, 'tensor', split_axis=1, concat_axis=1, axis_index_...  6.77 us
    pallas_call x1, Pallas kernels, backward_of(): pl.pallas_call(backward_kernel, out_shape=jax.ShapeDtypeStruct((heads, co...  5.51 us
    pallas_call x2, Pallas kernels, forward_of(): pl.pallas_call(functools.partial(forward_kernel, head), out_shape=jax.Sha...  4.58 us
    ppermute x2, starting transfers between devices, passed_along(): return lax.ppermute(block, 'pipe', route)  4.01 us
    unnamed x11, local copies, waits for them, and re-layouts  3.94 us
  transfers between devices with their start and end apart: 8, of which 2 were waited for; matrix products, arithmetic and copies ran while one was open for 7% of the time, Pallas kernels for 10%

profile of v5, /device:TPU:48, one launch (start us, length us, event | category | flops | bytes accessed | tf_op | source)
XLA Modules:
  0.0 104.4 jit_solution(15275675255473492094)
XLA Ops:
  0.7 2.3 %constant_dynamic-slice_fusion.1 = (bf16[1,56,8,384]{3,2,1,0:T(8,128)(2,1)S(1)}, bf16[448,384]{1,0:T(8,128)(2,1)}, bf16[448,384]{1,0:T(8,128)(2,1)}, bf16[1,56,8,384]{3,2,1,0:T(8,128)(2,1)S(1)}) fusion(bf16[1,56,32,384]{3,2,1,0:T(8,128)(2,1)} %param.6, s32[]{:T(128)S(6)} %select_n.41, s32[]{:T(128)S(6)} %select_n.39, s32[]{:T(128)S(6)} %select_n.37, ...), kind=kLoop, calls=%fused_computation.9 | loop fusion | bytes 2752528 | tf_op jit(solution)/shard_map/dynamic_slice | solution.py:202
  3.1 0.0 copy-start.2
  3.1 0.9 maximum_bitcast_fusion
  4.0 4.3 %all-to-all-start.1 = ((bf16[2,4,2,56,384]{4,3,2,0,1:T(8,128)(2,1)}), bf16[2,4,2,56,384]{4,3,2,0,1:T(8,128)(2,1)S(1)}, u32[]{:S(2)}, u32[]{:S(2)}) async-start(bf16[2,4,2,56,384]{4,3,2,0,1:T(8,128)(2,1)} %maximum_bitcast_fusion), calls=%async_computation.1 | async-start | bytes 1376256 | tf_op jit(solution)/shard_map/all_to_all | solution.py:188
  8.3 14.3 %collective-permute-start.3 = (bf16[448,384]{1,0:T(8,128)(2,1)}, bf16[448,384]{1,0:T(8,128)(2,1)S(1)}, u32[]{:S(2)}, u32[]{:S(2)}) collective-permute-start(bf16[448,384]{1,0:T(8,128)(2,1)} %get-tuple-element.13), channel_id=1, source_target_pairs={{0,488},{1,489},{2,490},{3,491},{4,492},{5,493},{6,494},{7,495},{8... | collective-permute-start | bytes 1032200 | tf_op jit(solution)/shard_map/ppermute | solution.py:182
  22.6 0.0 copy-start
  22.6 0.0 copy-start.1
  22.6 3.9 %collective-permute-start.2 = (bf16[448,384]{1,0:T(8,128)(2,1)}, bf16[448,384]{1,0:T(8,128)(2,1)S(1)}, u32[]{:S(2)}, u32[]{:S(2)}) collective-permute-start(bf16[448,384]{1,0:T(8,128)(2,1)} %get-tuple-element.14), channel_id=1, source_target_pairs={{0,480},{1,481},{2,482},{3,483},{4,484},{5,485},{6,486},{7,487},{8... | collective-permute-start | bytes 1032200 | tf_op jit(solution)/shard_map/ppermute | solution.py:182
  26.6 0.0 copy-done.2
  26.6 0.2 copy.36
  26.8 0.0 copy-done
  26.8 0.0 copy-done.1
  26.8 2.3 %forward_attention.3 = bf16[896,128]{1,0:T(8,128)(2,1)S(1)} custom-call(s32[1,2]{1,0:T(1,128)S(1)} %copy-done.1, s32[4,896]{1,0:T(4,128)S(1)} %copy-done, bf16[2,896,384]{2,1,0:T(8,128)(2,1)S(1)} %bitcast.40), custom_call_target="tpu_custom_call" | custom-call | flops 49999998976 | tf_op jit(solution)/shard_map/forward_attention/pallas_call | solution.py:123
  29.1 0.0 copy-start.3
  29.1 2.3 %forward_attention.2 = bf16[896,128]{1,0:T(8,128)(2,1)S(1)} custom-call(s32[1,2]{1,0:T(1,128)S(1)} %copy-done.1, s32[4,896]{1,0:T(4,128)S(1)} %copy-done, bf16[2,896,384]{2,1,0:T(8,128)(2,1)S(1)} %bitcast.41), custom_call_target="tpu_custom_call" | custom-call | flops 49999998976 | tf_op jit(solution)/shard_map/forward_attention/pallas_call | solution.py:123
  31.4 0.6 slice.10
  32.1 0.0 copy-done.3
  32.1 0.1 copy.37
  32.2 0.7 concatenate.4
  32.9 1.9 %collective-permute-start = (bf16[2,912,128]{2,1,0:T(8,128)(2,1)S(1)}, bf16[2,912,128]{2,1,0:T(8,128)(2,1)S(1)}, u32[]{:S(2)}, u32[]{:S(2)}) collective-permute-start(bf16[2,912,128]{2,1,0:T(8,128)(2,1)S(1)} %concatenate.4), channel_id=1, source_target_pairs={{16,0},{32,16},{48,32},{64,48},{80,64},{96,80},{112,96},{128,112},... | collective-permute-start | bytes 1400840 | tf_op jit(solution)/shard_map/ppermute | solution.py:172
  34.8 0.0 all-to-all-done.1
  34.8 0.9 slice_bitcast_fusion
  35.8 5.2 %collective-permute-start.5 = (bf16[4,2,56,384]{3,2,1,0:T(8,128)(2,1)}, bf16[4,2,56,384]{3,2,1,0:T(8,128)(2,1)S(1)}, u32[]{:S(2)}, u32[]{:S(2)}) collective-permute-start(bf16[4,2,56,384]{3,2,1,0:T(8,128)(2,1)} %get-tuple-element.16), channel_id=1, source_target_pairs={{0,484},{1,485},{2,486},{3,487},{4,488},{5,489},{6,490},{7,491},{8... | collective-permute-start | bytes 1032200 | tf_op jit(solution)/shard_map/ppermute | solution.py:182
  40.9 4.6 %collective-permute-start.4 = (bf16[4,2,56,384]{3,2,1,0:T(8,128)(2,1)}, bf16[4,2,56,384]{3,2,1,0:T(8,128)(2,1)S(1)}, u32[]{:S(2)}, u32[]{:S(2)}) collective-permute-start(bf16[4,2,56,384]{3,2,1,0:T(8,128)(2,1)} %get-tuple-element.17), channel_id=1, source_target_pairs={{0,492},{1,493},{2,494},{3,495},{4,480},{5,481},{6,482},{7,483},{8... | collective-permute-start | bytes 1032200 | tf_op jit(solution)/shard_map/ppermute | solution.py:182
  45.5 0.0 collective-permute-done.3.refs_1_
  45.5 34.2 %collective-permute-done.2.refs_0_ = bf16[448,384]{1,0:T(8,128)(2,1)S(1)} collective-permute-done((bf16[448,384]{1,0:T(8,128)(2,1)}, bf16[448,384]{1,0:T(8,128)(2,1)S(1)}, u32[]{:S(2)}, u32[]{:S(2)}) %collective-permute-start.2) | collective-permute-done | bytes 344096 | tf_op jit(solution)/shard_map/ppermute | solution.py:182
  79.8 0.1 stacked.2
  79.8 0.7 copy.23
  80.5 1.0 copy.24
  81.5 4.5 %all-to-all-start = ((bf16[2,4,2,56,384]{4,3,2,0,1:T(8,128)(2,1)}), bf16[2,4,2,56,384]{4,3,2,0,1:T(8,128)(2,1)S(1)}, u32[]{:S(2)}, u32[]{:S(2)}) async-start(bf16[2,4,2,56,384]{4,3,2,0,1:T(8,128)(2,1)} %copy.24), calls=%async_computation | async-start | bytes 1376256 | tf_op jit(solution)/shard_map/all_to_all | solution.py:188
  86.1 0.0 collective-permute-done.grad_ref
  86.1 2.1 %collective-permute-start.1 = (bf16[2,896,128]{2,1,0:T(8,128)(2,1)S(1)}, bf16[2,896,128]{2,1,0:T(8,128)(2,1)S(1)}, u32[]{:S(2)}, u32[]{:S(2)}) collective-permute-start(bf16[2,896,128]{2,1,0:T(8,128)(2,1)S(1)} %pad_maximum_fusion), channel_id=1, source_target_pairs={{0,16},{16,32},{32,48},{48,64},{64,80},{80,96},{96,112},{112,128},... | collective-permute-start | bytes 1376264 | tf_op jit(solution)/shard_map/ppermute | solution.py:172
  88.2 0.0 collective-permute-done.5.refs_1_
  88.2 0.0 collective-permute-done.4.refs_0_
  88.2 0.1 stacked.3.late_ref
  88.3 6.8 %all-to-all-done = bf16[2,4,2,56,384]{4,3,2,0,1:T(8,128)(2,1)S(1)} async-done(((bf16[2,4,2,56,384]{4,3,2,0,1:T(8,128)(2,1)}), bf16[2,4,2,56,384]{4,3,2,0,1:T(8,128)(2,1)S(1)}, u32[]{:S(2)}, u32[]{:S(2)}) %all-to-all-start) | async-done | bytes 688160 | tf_op jit(solution)/shard_map/all_to_all | solution.py:188
  95.0 0.1 copy.29.early_ref
  95.1 5.5 %backward_attention.1 = bf16[2,896,384]{2,1,0:T(8,128)(2,1)S(1)} custom-call(s32[1]{0:T(128)} %bitcast.10.place_ref, s32[4,896]{1,0:T(4,128)S(1)} %copy-done, bf16[2,912,128]{2,1,0:T(8,128)(2,1)S(1)} %collective-permute-done.grad_ref, bf16[2,4,2,56,384]{4,3,2,1,0:T(8,128)(2,1)S(1)} %copy.29.early_ref, bf16[2,4,2,56,384]{4,3,2,1,0:T(8,128)(2,1)S(1)} %stacked.3.late_ref), custom_call_target="tpu_custom_call" | custom-call | tf_op jit(solution)/shard_map/backward_attention/pallas_call | solution.py:137
  100.6 2.5 %copy.31 = bf16[1,896,2,384]{3,2,1,0:T(2,128)(2,1)} copy(bf16[1,896,2,384]{3,1,2,0:T(8,128)(2,1)S(1)} %bitcast.39) | data formatting | bytes 2752512
  103.1 0.0 collective-permute-done.1
  103.1 1.2 %copy.30 = bf16[1,896,2,128]{3,2,1,0:T(2,128)(2,1)} copy(bf16[1,896,2,128]{3,1,2,0:T(8,128)(2,1)S(1)} %bitcast.48) | data formatting | bytes 917504
  (4 shorter events, 0.1 us)
Async XLA Ops:
  3.1 23.5 %copy-start.2 = (bf16[1,896,2,384]{3,2,1,0:T(2,128)(2,1)S(1)}, bf16[1,896,2,384]{3,2,1,0:T(2,128)(2,1)}, u32[]{:S(2)}) copy-start(bf16[1,896,2,384]{3,2,1,0:T(2,128)(2,1)} %param.5) | copy-start | bytes 4128772
  4.0 30.8 %all-to-all-start.1 = ((bf16[2,4,2,56,384]{4,3,2,0,1:T(8,128)(2,1)}), bf16[2,4,2,56,384]{4,3,2,0,1:T(8,128)(2,1)S(1)}, u32[]{:S(2)}, u32[]{:S(2)}) async-start(bf16[2,4,2,56,384]{4,3,2,0,1:T(8,128)(2,1)} %maximum_bitcast_fusion), calls=%async_computation.1 | async-start | bytes 1376256 | tf_op jit(solution)/shard_map/all_to_all | solution.py:188
  8.3 37.2 %collective-permute-start.3 = (bf16[448,384]{1,0:T(8,128)(2,1)}, bf16[448,384]{1,0:T(8,128)(2,1)S(1)}, u32[]{:S(2)}, u32[]{:S(2)}) collective-permute-start(bf16[448,384]{1,0:T(8,128)(2,1)} %get-tuple-element.13), channel_id=1, source_target_pairs={{0,488},{1,489},{2,490},{3,491},{4,492},{5,493},{6,494},{7,495},{8... | collective-permute-start | bytes 1032200 | tf_op jit(solution)/shard_map/ppermute | solution.py:182
  22.6 4.2 %copy-start = (s32[4,896]{1,0:T(4,128)S(1)}, s32[4,896]{1,0:T(4,128)}, u32[]{:S(2)}) copy-start(s32[4,896]{1,0:T(4,128)} %pos_ref.5) | copy-start | bytes 43012
  22.6 4.2 %copy-start.1 = (s32[1,2]{1,0:T(1,128)S(1)}, s32[1,2]{1,0:T(1,128)}, u32[]{:S(2)}) copy-start(s32[1,2]{1,0:T(1,128)} %which_ref.3) | copy-start | bytes 28
  22.6 57.1 %collective-permute-start.2 = (bf16[448,384]{1,0:T(8,128)(2,1)}, bf16[448,384]{1,0:T(8,128)(2,1)S(1)}, u32[]{:S(2)}, u32[]{:S(2)}) collective-permute-start(bf16[448,384]{1,0:T(8,128)(2,1)} %get-tuple-element.14), channel_id=1, source_target_pairs={{0,480},{1,481},{2,482},{3,483},{4,484},{5,485},{6,486},{7,487},{8... | collective-permute-start | bytes 1032200 | tf_op jit(solution)/shard_map/ppermute | solution.py:182
  29.1 3.0 %copy-start.3 = (bf16[1,896,2,128]{3,2,1,0:T(2,128)(2,1)S(1)}, bf16[1,896,2,128]{3,2,1,0:T(2,128)(2,1)}, u32[]{:S(2)}) copy-start(bf16[1,896,2,128]{3,2,1,0:T(2,128)(2,1)} %param.7) | copy-start | bytes 1376260
  32.9 53.2 %collective-permute-start = (bf16[2,912,128]{2,1,0:T(8,128)(2,1)S(1)}, bf16[2,912,128]{2,1,0:T(8,128)(2,1)S(1)}, u32[]{:S(2)}, u32[]{:S(2)}) collective-permute-start(bf16[2,912,128]{2,1,0:T(8,128)(2,1)S(1)} %concatenate.4), channel_id=1, source_target_pairs={{16,0},{32,16},{48,32},{64,48},{80,64},{96,80},{112,96},{128,112},... | collective-permute-start | bytes 1400840 | tf_op jit(solution)/shard_map/ppermute | solution.py:172
  35.8 52.4 %collective-permute-start.5 = (bf16[4,2,56,384]{3,2,1,0:T(8,128)(2,1)}, bf16[4,2,56,384]{3,2,1,0:T(8,128)(2,1)S(1)}, u32[]{:S(2)}, u32[]{:S(2)}) collective-permute-start(bf16[4,2,56,384]{3,2,1,0:T(8,128)(2,1)} %get-tuple-element.16), channel_id=1, source_target_pairs={{0,484},{1,485},{2,486},{3,487},{4,488},{5,489},{6,490},{7,491},{8... | collective-permute-start | bytes 1032200 | tf_op jit(solution)/shard_map/ppermute | solution.py:182
  40.9 47.3 %collective-permute-start.4 = (bf16[4,2,56,384]{3,2,1,0:T(8,128)(2,1)}, bf16[4,2,56,384]{3,2,1,0:T(8,128)(2,1)S(1)}, u32[]{:S(2)}, u32[]{:S(2)}) collective-permute-start(bf16[4,2,56,384]{3,2,1,0:T(8,128)(2,1)} %get-tuple-element.17), channel_id=1, source_target_pairs={{0,492},{1,493},{2,494},{3,495},{4,480},{5,481},{6,482},{7,483},{8... | collective-permute-start | bytes 1032200 | tf_op jit(solution)/shard_map/ppermute | solution.py:182
  81.5 13.5 %all-to-all-start = ((bf16[2,4,2,56,384]{4,3,2,0,1:T(8,128)(2,1)}), bf16[2,4,2,56,384]{4,3,2,0,1:T(8,128)(2,1)S(1)}, u32[]{:S(2)}, u32[]{:S(2)}) async-start(bf16[2,4,2,56,384]{4,3,2,0,1:T(8,128)(2,1)} %copy.24), calls=%async_computation | async-start | bytes 1376256 | tf_op jit(solution)/shard_map/all_to_all | solution.py:188
  86.1 17.1 %collective-permute-start.1 = (bf16[2,896,128]{2,1,0:T(8,128)(2,1)S(1)}, bf16[2,896,128]{2,1,0:T(8,128)(2,1)S(1)}, u32[]{:S(2)}, u32[]{:S(2)}) collective-permute-start(bf16[2,896,128]{2,1,0:T(8,128)(2,1)S(1)} %pad_maximum_fusion), channel_id=1, source_target_pairs={{0,16},{16,32},{32,48},{48,64},{64,80},{80,96},{96,112},{112,128},... | collective-permute-start | bytes 1376264 | tf_op jit(solution)/shard_map/ppermute | solution.py:172
